TPU v7x, 32 devices: a whole 2x2x4 slice. The times are simulated.
32 devices in a mesh: gx: 4 (over x, core), gy: 8 (over z, y).
Axes of the slice: x: 2, y: 2, z: 4, core: 2. Of those that a mesh axis runs over, the one named last changes fastest.
Arguments:
- values: float32 [8192, 128], P(('gx', 'gy')), may hold values from -6 to 6
- noise: float32 [8192, 128], P(('gx', 'gy')), may hold values from 0.1 to 1
- fractions: float32 [3, 8192, 128], P(None, ('gx', 'gy')), may hold values from 0 to 1
- cell_xy: int32 [2, 8192, 128], P(None, ('gx', 'gy')), may hold values from 0 to 7
- cell_z: int32 [8192, 128], P(('gx', 'gy')), may hold values from 0 to 255
- tile_grid: int32 [8192], P(('gx', 'gy')), may hold values from 0 to 127
- counts: int32 [8192], P(('gx', 'gy')), may hold values from 1 to 128, as said below
- rate_x: float32 [512], replicated, may hold values from 0.01 to 4
- rate_y: float32 [512], replicated, may hold values from 0.01 to 4
- rate_z: float32 [256], replicated, may hold values from 0.01 to 4
Outputs:
- product: float32 [8192, 128], P(('gx', 'gy'))
Inputs may be any that keep to these rules, and one draw needn't show every extreme that they name: `counts`: every fifth point tile, counted from tile 0, is full. `tile_grid`: A point tile's grid tile is numbered within its own device's block of the grid.
All inputs are finite; a program needn't handle non-finite values.
Results may differ from a plain program's by a relative error of at most 0.00005.
Values sent between devices are 32-bit elements; how exact they have to be, the bound alone decides.
A program may use at most 128 MiB of HBM per device.

v0:
```python
import math

import jax
import jax.numpy as jnp
from jax import lax
from jax.sharding import PartitionSpec as P

TILE = 8


PRECISE = lax.Precision.HIGHEST


def extended(block, sides, width):
    for axis, dim in sides:
        count = lax.axis_size(axis)
        forward = [(i, i + 1) for i in range(count - 1)]
        forward.append((count - 1, 0))
        backward = [(target, source) for source, target in forward]
        low = lax.ppermute(
            lax.slice_in_dim(block, block.shape[dim] - width, None, axis=dim), axis, forward
        )
        high = lax.ppermute(lax.slice_in_dim(block, 0, width, axis=dim), axis, backward)
        block = jnp.concatenate([low, block, high], axis=dim)
    return block


def cubic_taps(fraction):
    square = fraction * fraction
    cubed = square * fraction
    return (
        -0.5 * cubed + square - 0.5 * fraction,
        1.5 * cubed - 2.5 * square + 1.0,
        -1.5 * cubed + 2.0 * square + 0.5 * fraction,
        0.5 * cubed - 0.5 * square,
    )


def cas_table(length):
    counter = jnp.arange(length, dtype=jnp.int32)
    phase_mod = counter[:, None] * counter[None, :] % length
    radians = phase_mod.astype(jnp.float32) * (2.0 * math.pi / length)
    return jnp.cos(radians) + jnp.sin(radians)


def dense_weights(taps, start, length, periodic):
    box_span = jnp.arange(length, dtype=jnp.int32)
    weight_sum = jnp.zeros(start.shape + (length,), jnp.float32)
    for offset in range(4):
        position = start + offset
        if periodic:
            position = position % length
        weight_sum = weight_sum + jnp.where(
            position[..., None] == box_span, taps[offset][..., None], 0.0
        )
    return weight_sum


def body(values, noise, fractions, cell_xy, cell_z, tile_grid, counts, rate_x, rate_y, rate_z):
    tile_count, point_count = values.shape
    ranks_x = lax.axis_size("gx")
    ranks_y = lax.axis_size("gy")
    full_x = rate_x.shape[0]
    full_y = rate_y.shape[0]
    depth = rate_z.shape[0]
    cells_x = full_x // ranks_x
    cells_y = full_y // ranks_y
    rows_x = cells_x // TILE
    rows_y = cells_y // TILE
    grid_tiles = rows_x * rows_y
    box_side = TILE + 4
    tile_block = math.gcd(tile_count, 64)
    block_count = tile_count // tile_block
    is_live = jnp.arange(point_count, dtype=jnp.int32)[None, :] < counts[:, None]
    source = jnp.where(is_live, values, 0.0)
    catalog = jnp.arange(grid_tiles, dtype=jnp.int32)

    def blocked(array):
        return array.reshape((block_count, tile_block) + array.shape[1:])

    tile_items = (
        blocked(fractions[0]),
        blocked(fractions[1]),
        blocked(fractions[2]),
        blocked(cell_xy[0]),
        blocked(cell_xy[1]),
        blocked(cell_z),
        blocked(tile_grid),
        blocked(source),
    )

    def tile_weights(tile_item):
        frac_x, frac_y, frac_z, start_x, start_y, start_z, owner_tile, block_source = tile_item
        wide_x = dense_weights(cubic_taps(frac_x), start_x + 1, box_side, False)
        wide_y = dense_weights(cubic_taps(frac_y), start_y + 1, box_side, False)
        plane_weight = (wide_x[..., :, None] * wide_y[..., None, :]).reshape(
            frac_x.shape + (box_side * box_side,)
        )
        column_weight = dense_weights(cubic_taps(frac_z), start_z - 1, depth, True)
        selector = (owner_tile[:, None] == catalog[None, :]).astype(jnp.float32)
        return (plane_weight, column_weight, selector, block_source)

    def spread_step(accum, tile_item):
        plane_weight, column_weight, selector, block_source = tile_weights(tile_item)
        tile_boxes = jnp.einsum(
            "bpq,bpz->bqz", plane_weight, column_weight * block_source[..., None], precision=PRECISE
        )
        return (accum + jnp.einsum("bg,bqz->gqz", selector, tile_boxes, precision=PRECISE), None)

    accum_start = jnp.zeros((grid_tiles, box_side * box_side, depth), jnp.float32)
    accum, _ = lax.scan(spread_step, accum_start, tile_items)
    cubes = accum.reshape(rows_x, rows_y, box_side, box_side, depth).transpose(0, 2, 1, 3, 4)
    leading = cubes[:, :TILE].reshape(cells_x, rows_y, box_side, depth)
    trailing = jnp.pad(cubes[:, TILE:], ((0, 0), (0, TILE - 4), (0, 0), (0, 0), (0, 0))).reshape(
        cells_x, rows_y, box_side, depth
    )
    strips = (
        jnp.pad(leading, ((0, 4), (0, 0), (0, 0), (0, 0)))
        + jnp.pad(trailing, ((TILE, 0), (0, 0), (0, 0), (0, 0)))[: cells_x + 4]
    )
    leading = strips[:, :, :TILE].reshape(cells_x + 4, cells_y, depth)
    trailing = jnp.pad(strips[:, :, TILE:], ((0, 0), (0, 0), (0, TILE - 4), (0, 0))).reshape(
        cells_x + 4, cells_y, depth
    )
    padded = (
        jnp.pad(leading, ((0, 0), (0, 4), (0, 0)))
        + jnp.pad(trailing, ((0, 0), (TILE, 0), (0, 0)))[:, : cells_y + 4]
    )
    widened = extended(padded, (("gx", 0), ("gy", 1)), 2)
    folded = jnp.concatenate(
        [
            widened[4:6] + widened[0:2],
            widened[6 : cells_x + 2],
            widened[cells_x + 2 : cells_x + 4] + widened[cells_x + 6 : cells_x + 8],
        ],
        0,
    )
    spread_grid = jnp.concatenate(
        [
            folded[:, 4:6] + folded[:, 0:2],
            folded[:, 6 : cells_y + 2],
            folded[:, cells_y + 2 : cells_y + 4] + folded[:, cells_y + 6 : cells_y + 8],
        ],
        1,
    )
    table_x = cas_table(full_x)
    table_y = cas_table(full_y)
    table_z = cas_table(depth)
    planes_dev = depth // (ranks_x * ranks_y)
    turned = jnp.einsum("xyz,zk->xky", spread_grid, table_z, precision=PRECISE)
    pencils = lax.all_to_all(turned, "gy", split_axis=1, concat_axis=2, tiled=True)
    pencils = jnp.einsum("xzy,yk->xzk", pencils, table_y, precision=PRECISE)
    planes = lax.all_to_all(pencils, "gx", split_axis=1, concat_axis=0, tiled=True)
    z_start = lax.axis_index("gy") * (depth // ranks_y) + lax.axis_index("gx") * planes_dev
    planes = jnp.einsum("xzy,xk->kzy", planes, table_x, precision=PRECISE)
    local_rate = lax.dynamic_slice_in_dim(rate_z, z_start, planes_dev)
    denom = 1.0 + rate_x[:, None, None] + rate_y[None, None, :] + local_rate[None, :, None]
    weighted = planes * (4.0 / (denom * denom))
    inverse = jnp.einsum("kzy,kx->xzy", weighted, table_x, precision=PRECISE)
    slabs = lax.all_to_all(inverse, "gx", split_axis=0, concat_axis=1, tiled=True)
    slabs = jnp.einsum("xzy,yk->xzk", slabs, table_y, precision=PRECISE)
    returned = lax.all_to_all(slabs, "gy", split_axis=2, concat_axis=1, tiled=True)
    grid_field = jnp.einsum("xzy,zk->xyk", returned, table_z, precision=PRECISE)
    grid_field = grid_field / (full_x * full_y * depth)
    bordered = extended(grid_field, (("gx", 0), ("gy", 1)), 2)
    leading = bordered[:cells_x].reshape(rows_x, TILE, cells_y + 4, depth)
    trailing = jnp.pad(bordered[TILE:], ((0, 4), (0, 0), (0, 0))).reshape(
        rows_x, TILE, cells_y + 4, depth
    )[:, :4]
    strips = jnp.concatenate([leading, trailing], 1)
    leading = strips[:, :, :cells_y].reshape(rows_x, box_side, rows_y, TILE, depth)
    trailing = jnp.pad(strips[:, :, TILE:], ((0, 0), (0, 0), (0, 4), (0, 0))).reshape(
        rows_x, box_side, rows_y, TILE, depth
    )[:, :, :, :4]
    grid_boxes = (
        jnp.concatenate([leading, trailing], 3)
        .transpose(0, 2, 1, 3, 4)
        .reshape(grid_tiles, box_side * box_side, depth)
    )

    def sample_step(carry, tile_item):
        plane_weight, column_weight, selector, block_source = tile_weights(tile_item)
        local_boxes = jnp.einsum("bg,gqz->bqz", selector, grid_boxes, precision=PRECISE)
        along_z = jnp.einsum("bpq,bqz->bpz", plane_weight, local_boxes, precision=PRECISE)
        return (carry, jnp.sum(along_z * column_weight, axis=-1))

    _, sampled = lax.scan(sample_step, None, tile_items)
    sampled = sampled.reshape(tile_count, point_count)
    return jnp.where(is_live, noise * values + sampled, 0.0)


def solution(mesh):
    in_specs = (
        P(("gx", "gy"), None),
        P(("gx", "gy"), None),
        P(None, ("gx", "gy"), None),
        P(None, ("gx", "gy"), None),
        P(("gx", "gy"), None),
        P(("gx", "gy")),
        P(("gx", "gy")),
        P(),
        P(),
        P(),
    )
    out_specs = P(("gx", "gy"), None)
    return jax.shard_map(body, mesh=mesh, in_specs=in_specs, out_specs=out_specs, check_vma=False)
```

profile of v0, /device:TPU:0, one launch (start us, length us, event | category | flops | bytes accessed | tf_op | source)
XLA Modules:
  0.0 1369.8 jit_solution(3926867960348072819)
XLA Ops:
  3.8 198.2 %while.33 = (s32[]{:T(128)}, f32[128,144,256]{2,0,1:T(8,128)}, s32[4,64]{1,0:T(4,128)S(1)}, s32[4,64,128]{2,1,0:T(8,128)S(1)}, f32[4,64,128]{2,1,0:T(8,128)S(1)}...) while((s32[]{:T(128)}, f32[128,144,256]{2,0,1:T(8,128)}, ...), condition=%wide.region_1.2_spmd.clone, body=%wide.region_0.1_spmd.clone.sunk | while | flops 7286579200 | bytes 69501848 | solution.py:111
  5.7 26.4 %fusion.201 = f32[64,144,256]{2,1,0:T(8,128)} fusion(f32[64,128,144]{1,0,2:T(8,128)S(1)} %bitcast.307, f32[64,128]{1,0:T(8,128)S(1)} %dynamic-slice_bitcast_fusion.2, f32[64,128]{1,0:T(8,128)S(1)} %get-tuple-element.941, s32[64,128]{1,0:T(8,128)S(1)} %get-tuple-element.942, f32[64,128]{1,0:T(8,128)S(1)} %get-tuple-element.943, ...), kind=kOutput, calls=%fused_computation.94.clone.2 | convolution fusion | flops 3649044480 | bytes 14450688 | tf_op jit(solution)/shard_map/while/body/eval_jaxpr/bpq,bpz->bqz/dot_general | solution.py:105
  32.1 19.2 %select_add_fusion.14 = f32[128,144,256]{2,0,1:T(8,128)} fusion(f32[128,144,256]{2,0,1:T(8,128)} %get-tuple-element.962, f32[64,144,256]{2,1,0:T(8,128)} %fusion.201, pred[]{:T(512)S(6)} %compare.53, s32[64]{0:T(128)S(1)} %fusion.202), kind=kOutput, calls=%fused_computation.91.clone.1 | convolution fusion | flops 3633324032 | bytes 47186176 | tf_op jit(solution)/shard_map/while/body/eval_jaxpr/bg,bqz->gqz/dot_general | solution.py:108
  53.2 26.4 %fusion.201 = f32[64,144,256]{2,1,0:T(8,128)} fusion(f32[64,128,144]{1,0,2:T(8,128)S(1)} %bitcast.307, f32[64,128]{1,0:T(8,128)S(1)} %dynamic-slice_bitcast_fusion.2, f32[64,128]{1,0:T(8,128)S(1)} %get-tuple-element.941, s32[64,128]{1,0:T(8,128)S(1)} %get-tuple-element.942, f32[64,128]{1,0:T(8,128)S(1)} %get-tuple-element.943, ...), kind=kOutput, calls=%fused_computation.94.clone.2 | convolution fusion | flops 3649044480 | bytes 14450688 | tf_op jit(solution)/shard_map/while/body/eval_jaxpr/bpq,bpz->bqz/dot_general | solution.py:105
  79.6 21.9 %select_add_fusion.14 = f32[128,144,256]{2,0,1:T(8,128)} fusion(f32[128,144,256]{2,0,1:T(8,128)} %get-tuple-element.962, f32[64,144,256]{2,1,0:T(8,128)} %fusion.201, pred[]{:T(512)S(6)} %compare.53, s32[64]{0:T(128)S(1)} %fusion.202), kind=kOutput, calls=%fused_computation.91.clone.1 | convolution fusion | flops 3633324032 | bytes 47186176 | tf_op jit(solution)/shard_map/while/body/eval_jaxpr/bg,bqz->gqz/dot_general | solution.py:108
  103.4 26.4 %fusion.201 = f32[64,144,256]{2,1,0:T(8,128)} fusion(f32[64,128,144]{1,0,2:T(8,128)S(1)} %bitcast.307, f32[64,128]{1,0:T(8,128)S(1)} %dynamic-slice_bitcast_fusion.2, f32[64,128]{1,0:T(8,128)S(1)} %get-tuple-element.941, s32[64,128]{1,0:T(8,128)S(1)} %get-tuple-element.942, f32[64,128]{1,0:T(8,128)S(1)} %get-tuple-element.943, ...), kind=kOutput, calls=%fused_computation.94.clone.2 | convolution fusion | flops 3649044480 | bytes 14450688 | tf_op jit(solution)/shard_map/while/body/eval_jaxpr/bpq,bpz->bqz/dot_general | solution.py:105
  129.8 21.9 %select_add_fusion.14 = f32[128,144,256]{2,0,1:T(8,128)} fusion(f32[128,144,256]{2,0,1:T(8,128)} %get-tuple-element.962, f32[64,144,256]{2,1,0:T(8,128)} %fusion.201, pred[]{:T(512)S(6)} %compare.53, s32[64]{0:T(128)S(1)} %fusion.202), kind=kOutput, calls=%fused_computation.91.clone.1 | convolution fusion | flops 3633324032 | bytes 47186176 | tf_op jit(solution)/shard_map/while/body/eval_jaxpr/bg,bqz->gqz/dot_general | solution.py:108
  153.6 26.4 %fusion.201 = f32[64,144,256]{2,1,0:T(8,128)} fusion(f32[64,128,144]{1,0,2:T(8,128)S(1)} %bitcast.307, f32[64,128]{1,0:T(8,128)S(1)} %dynamic-slice_bitcast_fusion.2, f32[64,128]{1,0:T(8,128)S(1)} %get-tuple-element.941, s32[64,128]{1,0:T(8,128)S(1)} %get-tuple-element.942, f32[64,128]{1,0:T(8,128)S(1)} %get-tuple-element.943, ...), kind=kOutput, calls=%fused_computation.94.clone.2 | convolution fusion | flops 3649044480 | bytes 14450688 | tf_op jit(solution)/shard_map/while/body/eval_jaxpr/bpq,bpz->bqz/dot_general | solution.py:105
  180.0 21.9 %select_add_fusion.14 = f32[128,144,256]{2,0,1:T(8,128)} fusion(f32[128,144,256]{2,0,1:T(8,128)} %get-tuple-element.962, f32[64,144,256]{2,1,0:T(8,128)} %fusion.201, pred[]{:T(512)S(6)} %compare.53, s32[64]{0:T(128)S(1)} %fusion.202), kind=kOutput, calls=%fused_computation.91.clone.1 | convolution fusion | flops 3633324032 | bytes 47186176 | tf_op jit(solution)/shard_map/while/body/eval_jaxpr/bg,bqz->gqz/dot_general | solution.py:108
  206.4 10.8 slice.140
  217.2 6.8 copy.107
  224.0 13.6 pad_bitcast_fusion
  237.6 9.2 slice_add_fusion
  256.0 10.7 fusion.89
  280.5 9.7 collective-permute-done.2
  292.7 5.9 pad_maximum_fusion
  298.6 9.0 slice.146
  308.0 9.1 pad_maximum_fusion.2
  320.5 15.2 %fusion.110 = f32[128,256,64]{0,1,2:T(8,128)S(1)} fusion(f32[128,2,256]{2,0,1:T(8,128)S(1)} %get-tuple-element.717, f32[128,60,256]{2,0,1:T(8,128)S(1)} %slice-done.4, f32[128,2,256]{2,0,1:T(8,128)S(1)} %get-tuple-element.716), kind=kOutput, calls=%fused_computation.233 | convolution fusion | flops 6447628288 | bytes 16777216 | tf_op jit(solution)/shard_map/xyz,zk->xky/dot_general | solution.py:150
  340.6 187.5 %all_to_all.72 = f32[128,256,64]{0,2,1:T(8,128)S(1)} all-to-all(f32[128,256,64]{0,2,1:T(8,128)S(1)} %copy.82), channel_id=1, replica_groups=mesh['gx'=4,'gy'=8] {'gy'}, dimensions={1} | all-to-all | bytes 16777216 | tf_op jit(solution)/shard_map/all_to_all | solution.py:151
  529.8 35.2 %fusion.118 = f32[128,32,512]{2,0,1:T(8,128)} fusion(f32[128,32,512]{0,2,1:T(8,128)S(1)} %bitcast.313), kind=kOutput, calls=%fused_computation.242 | convolution fusion | flops 12888834048 | bytes 16777216 | tf_op jit(solution)/shard_map/xzy,yk->xzk/dot_general | solution.py:152
  565.0 5.8 all-to-all-start.1
  571.0 92.9 %all-to-all-done.1 = f32[128,32,512]{2,0,1:T(8,128)} async-done(((f32[128,32,512]{2,0,1:T(8,128)}), f32[128,32,512]{2,0,1:T(8,128)}, u32[]{:S(2)}, u32[]{:S(2)}) %all-to-all-start.1) | async-done | bytes 8388640 | tf_op jit(solution)/shard_map/all_to_all | solution.py:153
  663.9 8.2 copy.85
  672.2 28.4 %fusion.98 = f32[512,8,512]{2,0,1:T(8,128)S(1)} fusion(f32[512,8,512]{2,1,0:T(8,128)S(1)} %bitcast.314), kind=kOutput, calls=%fused_computation.221 | convolution fusion | flops 12888834048 | bytes 16777216 | tf_op jit(solution)/shard_map/xzy,xk->kzy/dot_general | solution.py:155
  700.5 22.1 %fusion.100 = f32[512,8,512]{2,0,1:T(8,128)} fusion(f32[512,8,512]{2,0,1:T(8,128)S(1)} %fusion.98, f32[8]{0:T(128)S(1)} %dynamic_slice.156, f32[512,512]{1,0:T(8,128)S(1)} %broadcast_add_fusion), kind=kOutput, calls=%fused_computation.223 | convolution fusion | flops 12897222656 | bytes 17825824 | tf_op jit(solution)/shard_map/kzy,kx->xzy/dot_general | solution.py:159
  722.6 8.6 copy.89
  731.3 95.9 %all_to_all.73 = f32[512,8,512]{2,1,0:T(8,128)S(1)} all-to-all(f32[512,8,512]{2,1,0:T(8,128)S(1)} %copy.89), channel_id=1, replica_groups=mesh['gx'=4,'gy'=8] {'gx'}, dimensions={0} | all-to-all | bytes 16777216 | tf_op jit(solution)/shard_map/all_to_all | solution.py:160
  832.0 19.8 %fusion.116 = f32[128,32,512]{2,0,1:T(8,128)} fusion(f32[128,32,512]{2,0,1:T(8,128)S(1)} %bitcast.316), kind=kOutput, calls=%fused_computation.240 | convolution fusion | flops 12888834048 | bytes 16777216 | tf_op jit(solution)/shard_map/xzy,yk->xzk/dot_general | solution.py:161
  851.8 10.2 copy.91
  862.0 186.8 %all_to_all.74 = f32[128,32,512]{0,1,2:T(8,128)S(1)} all-to-all(f32[128,32,512]{0,1,2:T(8,128)} %copy.91), channel_id=1, replica_groups=mesh['gx'=4,'gy'=8] {'gy'}, dimensions={2} | all-to-all | bytes 16777216 | tf_op jit(solution)/shard_map/all_to_all | solution.py:162
  1053.5 19.0 %broadcast_multiply_fusion.2 = f32[128,64,256]{2,0,1:T(8,128)S(1)} fusion(f32[128,256,64]{0,2,1:T(8,128)S(1)} %bitcast.318), kind=kOutput, calls=%fused_computation.229 | convolution fusion | flops 6445531136 | bytes 16777216 | tf_op jit(solution)/shard_map/xzy,zk->xyk/dot_general | solution.py:163
  1082.2 9.6 collective-permute-done.6
  1101.9 8.8 copy_dynamic-update-slice_fusion
  1117.4 11.3 slice.154
  1128.7 11.6 slice_bitcast_fusion
  1140.3 11.4 pad_bitcast_fusion.1
  1154.5 7.1 maximum_bitcast_fusion
  1161.6 13.1 copy.97
  1174.7 194.1 %while.32 = (s32[]{:T(128)}, f32[4,64,128]{2,1,0:T(8,128)S(1)}, s32[4,64,128]{2,1,0:T(8,128)}, f32[4,64,128]{2,1,0:T(8,128)}, s32[4,64,128]{2,1,0:T(8,128)}, /*i...) while((s32[]{:T(128)}, f32[4,64,128]{2,1,0:T(8,128)S(1)}, ...), condition=%wide.region_4.5_spmd.clone, body=%wide.region_2.4_spmd.clone.sunk | while | flops 7279230976 | bytes 50627460 | solution.py:187
  1179.6 11.2 fusion.193
  1190.8 32.5 %multiply_reduce_fusion.2 = f32[64,128]{1,0:T(8,128)S(1)} fusion(f32[64,128]{1,0:T(8,128)S(1)} %get-tuple-element.891, s32[64,128]{1,0:T(8,128)S(1)} %get-tuple-element.892, f32[64,128]{1,0:T(8,128)S(1)} %get-tuple-element.893, s32[64,128]{1,0:T(8,128)S(1)} %get-tuple-element.894, f32[64,128]{1,0:T(8,128)S(1)} %get-tuple-element.895, ...), kind=kOutput, calls=%fused_computation.4.clone.1 | convolution fusion | flops 3651133440 | bytes 14450688 | tf_op jit(solution)/shard_map/while/body/eval_jaxpr/bpq,bqz->bpz/dot_general | solution.py:184
  1228.1 11.2 fusion.193
  1239.3 32.5 %multiply_reduce_fusion.2 = f32[64,128]{1,0:T(8,128)S(1)} fusion(f32[64,128]{1,0:T(8,128)S(1)} %get-tuple-element.891, s32[64,128]{1,0:T(8,128)S(1)} %get-tuple-element.892, f32[64,128]{1,0:T(8,128)S(1)} %get-tuple-element.893, s32[64,128]{1,0:T(8,128)S(1)} %get-tuple-element.894, f32[64,128]{1,0:T(8,128)S(1)} %get-tuple-element.895, ...), kind=kOutput, calls=%fused_computation.4.clone.1 | convolution fusion | flops 3651133440 | bytes 14450688 | tf_op jit(solution)/shard_map/while/body/eval_jaxpr/bpq,bqz->bpz/dot_general | solution.py:184
  1276.6 11.2 fusion.193
  1287.8 32.5 %multiply_reduce_fusion.2 = f32[64,128]{1,0:T(8,128)S(1)} fusion(f32[64,128]{1,0:T(8,128)S(1)} %get-tuple-element.891, s32[64,128]{1,0:T(8,128)S(1)} %get-tuple-element.892, f32[64,128]{1,0:T(8,128)S(1)} %get-tuple-element.893, s32[64,128]{1,0:T(8,128)S(1)} %get-tuple-element.894, f32[64,128]{1,0:T(8,128)S(1)} %get-tuple-element.895, ...), kind=kOutput, calls=%fused_computation.4.clone.1 | convolution fusion | flops 3651133440 | bytes 14450688 | tf_op jit(solution)/shard_map/while/body/eval_jaxpr/bpq,bqz->bpz/dot_general | solution.py:184
  1325.2 11.2 fusion.193
  1336.3 32.5 %multiply_reduce_fusion.2 = f32[64,128]{1,0:T(8,128)S(1)} fusion(f32[64,128]{1,0:T(8,128)S(1)} %get-tuple-element.891, s32[64,128]{1,0:T(8,128)S(1)} %get-tuple-element.892, f32[64,128]{1,0:T(8,128)S(1)} %get-tuple-element.893, s32[64,128]{1,0:T(8,128)S(1)} %get-tuple-element.894, f32[64,128]{1,0:T(8,128)S(1)} %get-tuple-element.895, ...), kind=kOutput, calls=%fused_computation.4.clone.1 | convolution fusion | flops 3651133440 | bytes 14450688 | tf_op jit(solution)/shard_map/while/body/eval_jaxpr/bpq,bqz->bpz/dot_general | solution.py:184
  (161 shorter events, 110.3 us)
Async XLA Ops:
  202.1 0.7 copy-start.4
  202.1 0.7 copy-start.5
  202.1 0.8 copy-start.6
  202.1 0.8 copy-start.7
  202.1 0.8 copy-start.8
  202.1 0.8 copy-start.13
  217.2 6.8 copy-start.3
  266.7 26.0 %copy-start = (f32[132,68,256]{2,0,1:T(8,128)S(1)}, f32[132,68,256]{2,0,1:T(8,128)}, u32[]{:S(2)}) copy-start(f32[132,68,256]{2,0,1:T(8,128)} %fusion.89) | copy-start | bytes 27574276
  268.2 5.2 collective-permute-start
  268.7 6.0 collective-permute-start.1
  275.8 14.5 %collective-permute-start.2 = (f32[136,2,256]{2,0,1:T(8,128)S(1)}, f32[136,2,256]{2,0,1:T(8,128)S(1)}, u32[]{:S(2)}, u32[]{:S(2)}) collective-permute-start(f32[136,2,256]{2,0,1:T(8,128)S(1)} %get-tuple-element.714), channel_id=1, source_target_pairs={{0,1},{1,2},{2,3},{3,4},{4,5},{5,6},{6,7},{7,0},{8,9},{9,10},{10,1... | collective-permute-start | bytes 835592 | tf_op jit(solution)/shard_map/ppermute | solution.py:20
  277.3 15.4 %collective-permute-start.3 = (f32[136,2,256]{2,0,1:T(8,128)S(1)}, f32[136,2,256]{2,0,1:T(8,128)S(1)}, u32[]{:S(2)}, u32[]{:S(2)}) collective-permute-start(f32[136,2,256]{2,0,1:T(8,128)S(1)} %get-tuple-element.715), channel_id=1, source_target_pairs={{1,0},{2,1},{3,2},{4,3},{5,4},{6,5},{7,6},{0,7},{9,8},{10,9},{11,1... | collective-permute-start | bytes 835592 | tf_op jit(solution)/shard_map/ppermute | solution.py:23
  307.8 9.3 slice-start
  307.8 9.3 slice-start.1
  308.0 9.1 slice-start.2
  317.3 3.2 slice-start.4
  564.9 5.8 copy-start.15
  564.9 5.9 copy-start.14
  565.0 5.9 copy-start.12
  565.0 99.0 %all-to-all-start.1 = ((f32[128,32,512]{2,0,1:T(8,128)}), f32[128,32,512]{2,0,1:T(8,128)}, u32[]{:S(2)}, u32[]{:S(2)}) async-start(f32[128,32,512]{2,0,1:T(8,128)} %fusion.118), calls=%async_computation.1 | async-start | bytes 16777216 | tf_op jit(solution)/shard_map/all_to_all | solution.py:153
  1072.5 4.9 copy-start.2
  1072.6 4.8 collective-permute-start.4
  1072.6 4.8 collective-permute-start.5
  1077.5 14.4 %collective-permute-start.6 = (f32[132,2,256]{2,0,1:T(8,128)S(1)}, f32[132,2,256]{2,0,1:T(8,128)S(1)}, u32[]{:S(2)}, u32[]{:S(2)}) collective-permute-start(f32[132,2,256]{2,0,1:T(8,128)S(1)} %get-tuple-element.720), channel_id=1, source_target_pairs={{0,1},{1,2},{2,3},{3,4},{4,5},{5,6},{6,7},{7,0},{8,9},{9,10},{10,1... | collective-permute-start | bytes 811016 | tf_op jit(solution)/shard_map/ppermute | solution.py:20
  1079.0 15.1 %collective-permute-start.7 = (f32[132,2,256]{2,0,1:T(8,128)S(1)}, f32[132,2,256]{2,0,1:T(8,128)S(1)}, u32[]{:S(2)}, u32[]{:S(2)}) collective-permute-start(f32[132,2,256]{2,0,1:T(8,128)S(1)} %get-tuple-element.721), channel_id=1, source_target_pairs={{1,0},{2,1},{3,2},{4,3},{5,4},{6,5},{7,6},{0,7},{9,8},{10,9},{11,1... | collective-permute-start | bytes 811016 | tf_op jit(solution)/shard_map/ppermute | solution.py:23
  1098.3 3.6 copy-start.1
  1101.9 8.8 slice-start.3
  1151.7 2.8 slice-start.5
  1174.7 194.1 %copy-start.9 = (f32[256,128]{1,0:T(8,128)S(1)}, f32[256,128]{1,0:T(8,128)}, u32[]{:S(2)}) copy-start(f32[256,128]{1,0:T(8,128)} %param.14) | copy-start | bytes 393220
  1174.7 194.1 %copy-start.10 = (f32[256,128]{1,0:T(8,128)S(1)}, f32[256,128]{1,0:T(8,128)}, u32[]{:S(2)}) copy-start(f32[256,128]{1,0:T(8,128)} %param.15) | copy-start | bytes 393220
  1174.7 194.1 %copy-start.11 = (s32[256]{0:T(256)S(1)}, s32[256]{0:T(256)}, u32[]{:S(2)}) copy-start(s32[256]{0:T(256)} %param.20) | copy-start | bytes 3076
where the time goes:
time: 1380 us; the launch traced here: 1370 us
  matrix products  505 us (37%)
  blocking collectives  470 us (34%)
  local copies, waits for them, and re-layouts  177 us (13%)
  waiting for transfers between devices  124 us (9%)
  other arithmetic  73.6 us (5%)
  starting transfers between devices  19.6 us (1%)
    all_to_all x1, blocking collectives, body(): lax.all_to_all(turned, 'gy', split_axis=1, concat_axis=2, tiled=True)  187 us
    all_to_all x1, blocking collectives, body(): lax.all_to_all(slabs, 'gy', split_axis=2, concat_axis=1, tiled=True)  187 us
    dot_general x4, matrix products, sample_step(): jnp.einsum('bpq,bqz->bpz', plane_weight, local_boxes, precision=PRECISE)  130 us
    dot_general x4, matrix products, spread_step(): jnp.einsum('bpq,bpz->bqz', plane_weight, column_weight * block_source[......  106 us
    all_to_all x1, blocking collectives, body(): lax.all_to_all(inverse, 'gx', split_axis=0, concat_axis=1, tiled=True)  95.9 us
    all_to_all x1, waiting for transfers between devices, body(): lax.all_to_all(pencils, 'gx', split_axis=1, concat_axis=0, tiled=True)  92.9 us
    dot_general x4, matrix products, spread_step(): jnp.einsum('bg,bqz->gqz', selector, tile_boxes, precision=PRECISE)  84.9 us
    dot_general x4, matrix products, sample_step(): jnp.einsum('bg,gqz->bqz', selector, grid_boxes, precision=PRECISE)  44.6 us
  transfers between devices with their start and end apart: 9, of which 8 were waited for; matrix products, arithmetic and copies ran while one was open for 0% of the time, Pallas kernels for 0%

commit v1 on v0

v1 whole, which is shorter than its diff:
```python
import functools
import math

import jax
import jax.numpy as jnp
import numpy as np
from jax import lax
from jax.experimental import pallas as pl
from jax.experimental.pallas import tpu as pltpu
from jax.sharding import PartitionSpec as P

TILE = 8
SIDE = 11
WINDOW = 16
GROUP = 8
LOW = 1
HIGH = 2
VMEM_BYTES = 48 * 1024 * 1024


def ring(axis):
    count = lax.axis_size(axis)
    forward = [(i, (i + 1) % count) for i in range(count)]
    return forward, [(target, source) for source, target in forward]


def cubic_taps(fraction):
    square = fraction * fraction
    cubed = square * fraction
    return (
        -0.5 * cubed + square - 0.5 * fraction,
        1.5 * cubed - 2.5 * square + 1.0,
        -1.5 * cubed + 2.0 * square + 0.5 * fraction,
        0.5 * cubed - 0.5 * square,
    )


def cas_table(length):
    counter = np.arange(length, dtype=np.int64)
    radians = (counter[:, None] * counter[None, :] % length) * (2.0 * math.pi / length)
    return jnp.asarray((np.cos(radians) + np.sin(radians)).astype(np.float32))


def halves(array):
    top = array.astype(jnp.bfloat16)
    return top, (array - top.astype(jnp.float32)).astype(jnp.bfloat16)


def split_dot(left, right, dims):
    left_top, left_rest = halves(left)
    right_top, right_rest = halves(right)

    def dot(a, b):
        return lax.dot_general(a, b, (dims, ((), ())), preferred_element_type=jnp.float32)

    return dot(left_top, right_top) + (dot(left_top, right_rest) + dot(left_rest, right_top))


def box_weights(taps, start, row):
    delta = lax.broadcasted_iota(jnp.int32, (WINDOW, start.shape[1]), 0) - start[row : row + 1]
    weight = jnp.zeros(delta.shape, jnp.float32)
    for offset in range(4):
        weight = jnp.where(delta == offset, taps[offset][row : row + 1], weight)
    return weight


def column_weights(taps, start, row, depth):
    delta = lax.broadcasted_iota(jnp.int32, (depth, start.shape[1]), 0) - start[row : row + 1] + 1
    delta = jnp.where(delta < 0, delta + depth, delta)
    delta = jnp.where(delta >= depth, delta - depth, delta)
    weight = jnp.zeros(delta.shape, jnp.float32)
    for offset in range(4):
        weight = jnp.where(delta == offset, taps[offset][row : row + 1], weight)
    return weight


def group_rows(refs, first):
    return [ref[pl.ds(first, GROUP), :] for ref in refs]


def spread_kernel(
    rows_y, tile_grid, counts, values, fx, fy, fz, cx, cy, cz, padded
):
    depth = padded.shape[2]
    points = values.shape[1]
    padded[...] = jnp.zeros_like(padded)

    def step(index, carry):
        first = pl.multiple_of(index * GROUP, GROUP)
        value, f0, f1, f2, c0, c1, c2 = group_rows((values, fx, fy, fz, cx, cy, cz), first)
        taps_x, taps_y, taps_z = cubic_taps(f0), cubic_taps(f1), cubic_taps(f2)
        slot = lax.broadcasted_iota(jnp.int32, (1, points), 1)
        boxes = []
        for row in range(GROUP):
            source = jnp.where(slot < counts[first + row], value[row : row + 1], 0.0)
            wide_x = box_weights(taps_x, c0, row) * source
            wide_y = box_weights(taps_y, c1, row)
            plane = jnp.concatenate([wide_x[x : x + 1] * wide_y for x in range(SIDE)], 0)
            column = column_weights(taps_z, c2, row, depth)
            boxes.append(split_dot(plane, column, ((1,), (1,))))
        for row in range(GROUP):
            owner = tile_grid[first + row]
            at_x = (owner // rows_y) * TILE
            at_y = pl.multiple_of(lax.rem(owner, rows_y) * TILE, TILE)
            padded[pl.ds(at_x, SIDE), pl.ds(at_y, WINDOW), :] += boxes[row].reshape(
                SIDE, WINDOW, depth
            )
        return carry

    lax.fori_loop(0, values.shape[0] // GROUP, step, 0)


def sample_kernel(
    rows_y, tile_grid, counts, values, noise, fx, fy, fz, cx, cy, cz, field, product
):
    depth = field.shape[2]
    points = values.shape[1]

    def step(index, carry):
        first = pl.multiple_of(index * GROUP, GROUP)
        value, level, f0, f1, f2, c0, c1, c2 = group_rows(
            (values, noise, fx, fy, fz, cx, cy, cz), first
        )
        taps_x, taps_y, taps_z = cubic_taps(f0), cubic_taps(f1), cubic_taps(f2)
        slot = lax.broadcasted_iota(jnp.int32, (1, points), 1)
        rows = []
        for row in range(GROUP):
            owner = tile_grid[first + row]
            at_x = (owner // rows_y) * TILE
            at_y = pl.multiple_of(lax.rem(owner, rows_y) * TILE, TILE)
            box = field[pl.ds(at_x, SIDE), pl.ds(at_y, WINDOW), :].reshape(SIDE * WINDOW, depth)
            column = column_weights(taps_z, c2, row, depth)
            along = split_dot(box, column, ((1,), (0,))).reshape(SIDE, WINDOW, points)
            wide_x = box_weights(taps_x, c0, row)
            wide_y = box_weights(taps_y, c1, row)
            total = along[0] * wide_x[0:1]
            for x in range(1, SIDE):
                total = total + along[x] * wide_x[x : x + 1]
            sampled = jnp.sum(total * wide_y, axis=0, keepdims=True)
            result = level[row : row + 1] * value[row : row + 1] + sampled
            rows.append(jnp.where(slot < counts[first + row], result, 0.0))
        product[pl.ds(first, GROUP), :] = jnp.concatenate(rows, 0)
        return carry

    lax.fori_loop(0, values.shape[0] // GROUP, step, 0)


def body(values, noise, fractions, cell_xy, cell_z, tile_grid, counts, rate_x, rate_y, rate_z):
    tile_count, point_count = values.shape
    ranks_x = lax.axis_size("gx")
    ranks_y = lax.axis_size("gy")
    full_x = rate_x.shape[0]
    full_y = rate_y.shape[0]
    depth = rate_z.shape[0]
    cells_x = full_x // ranks_x
    cells_y = full_y // ranks_y
    rows_y = cells_y // TILE
    wide_x = cells_x + LOW + HIGH
    wide_y = cells_y + TILE
    smem = pl.BlockSpec(memory_space=pltpu.SMEM)
    vmem = pl.BlockSpec(memory_space=pltpu.VMEM)
    params = pltpu.CompilerParams(vmem_limit_bytes=VMEM_BYTES)
    places = (
        fractions[0], fractions[1], fractions[2], cell_xy[0], cell_xy[1], cell_z,
    )
    flops = 6 * tile_count * SIDE * WINDOW * point_count * depth
    cost = pl.CostEstimate(
        flops=flops, bytes_accessed=4 * wide_x * wide_y * depth, transcendentals=0
    )
    padded = pl.pallas_call(
        functools.partial(spread_kernel, rows_y),
        out_shape=jax.ShapeDtypeStruct((wide_x, wide_y, depth), jnp.float32),
        in_specs=[smem, smem] + [vmem] * 7,
        out_specs=vmem,
        compiler_params=params,
        cost_estimate=cost,
        name="spread",
    )(tile_grid, counts, values, *places)

    forward_x, backward_x = ring("gx")
    forward_y, backward_y = ring("gy")
    from_low = lax.ppermute(padded[cells_x + LOW :], "gx", forward_x)
    from_high = lax.ppermute(padded[:LOW], "gx", backward_x)
    padded = jnp.concatenate(
        [
            padded[LOW : LOW + HIGH] + from_low,
            padded[LOW + HIGH : cells_x],
            padded[cells_x : cells_x + LOW] + from_high,
        ],
        0,
    )
    from_low = lax.ppermute(
        padded[:, cells_y + LOW : cells_y + LOW + HIGH], "gy", forward_y
    )
    from_high = lax.ppermute(padded[:, :LOW], "gy", backward_y)
    spread_grid = jnp.concatenate(
        [
            padded[:, LOW : LOW + HIGH] + from_low,
            padded[:, LOW + HIGH : cells_y],
            padded[:, cells_y : cells_y + LOW] + from_high,
        ],
        1,
    )

    table_x = cas_table(full_x)
    table_y = cas_table(full_y)
    table_z = cas_table(depth)
    planes_dev = depth // (ranks_x * ranks_y)
    einsum = functools.partial(jnp.einsum, precision=lax.Precision.HIGH)
    turned = einsum("xyz,zk->xky", spread_grid, table_z)
    pencils = lax.all_to_all(turned, "gy", split_axis=1, concat_axis=2, tiled=True)
    pencils = einsum("xzy,yk->xzk", pencils, table_y)
    planes = lax.all_to_all(pencils, "gx", split_axis=1, concat_axis=0, tiled=True)
    z_start = lax.axis_index("gy") * (depth // ranks_y) + lax.axis_index("gx") * planes_dev
    planes = einsum("xzy,xk->kzy", planes, table_x)
    local_rate = lax.dynamic_slice_in_dim(rate_z, z_start, planes_dev)
    denom = 1.0 + rate_x[:, None, None] + rate_y[None, None, :] + local_rate[None, :, None]
    weighted = planes * ((4.0 / (full_x * full_y * depth)) / (denom * denom))
    inverse = einsum("kzy,kx->xzy", weighted, table_x)
    slabs = lax.all_to_all(inverse, "gx", split_axis=0, concat_axis=1, tiled=True)
    slabs = einsum("xzy,yk->xzk", slabs, table_y)
    returned = lax.all_to_all(slabs, "gy", split_axis=2, concat_axis=1, tiled=True)
    block = einsum("xzy,zk->xyk", returned, table_z)

    low = lax.ppermute(block[cells_x - LOW :], "gx", forward_x)
    high = lax.ppermute(block[:HIGH], "gx", backward_x)
    block = jnp.concatenate([low, block, high], 0)
    low = lax.ppermute(block[:, cells_y - LOW :], "gy", forward_y)
    high = lax.ppermute(block[:, :HIGH], "gy", backward_y)
    spare = jnp.zeros((wide_x, TILE - LOW - HIGH, depth), jnp.float32)
    field = jnp.concatenate([low, block, high, spare], 1)

    return pl.pallas_call(
        functools.partial(sample_kernel, rows_y),
        out_shape=jax.ShapeDtypeStruct((tile_count, point_count), jnp.float32),
        in_specs=[smem, smem] + [vmem] * 9,
        out_specs=vmem,
        compiler_params=params,
        cost_estimate=cost,
        name="sample",
    )(tile_grid, counts, values, noise, *places, field)


def solution(mesh):
    in_specs = (
        P(("gx", "gy"), None),
        P(("gx", "gy"), None),
        P(None, ("gx", "gy"), None),
        P(None, ("gx", "gy"), None),
        P(("gx", "gy"), None),
        P(("gx", "gy")),
        P(("gx", "gy")),
        P(),
        P(),
        P(),
    )
    out_specs = P(("gx", "gy"), None)
    return jax.shard_map(body, mesh=mesh, in_specs=in_specs, out_specs=out_specs, check_vma=False)
```

time: 1380 us -> 843 us (0.61)
  matrix products: 505 us -> 54.1 us
  local copies, waits for them, and re-layouts: 177 us -> 73.4 us
  Pallas kernels: 0 us -> 90.2 us
  other arithmetic: 73.6 us -> 16.8 us
  waiting for transfers between devices: 124 us -> 107 us
    dot_general x22 -> x6, matrix products: 505 us -> 54.1 us  [the longest x1 11.5 us: body(): planes = einsum('xzy,xk->kzy', planes, table_x)]
    pallas_call x0 -> x2, Pallas kernels: none -> 90.2 us  [the longest x1 45.9 us: body(): pl.pallas_call(functools.partial(spread_kernel, rows_y), out_shape=jax.Sh...]
    reshape x6 -> x0, local copies, waits for them, and re-layouts: 39.8 us -> none  [the longest x1 13.6 us: body(): jnp.pad(cubes[:, TILE:], ((0, 0), (0, TILE - 4), (0, 0), (0, 0), (0, 0)))]
    slice x17 -> x6, local copies, waits for them, and re-layouts: 49.8 us -> 10.9 us  [the longest x1 4.84 us: body(): padded[:, LOW + HIGH:cells_y]]
    add x29 -> x4, other arithmetic: 26 us -> 4.15 us  [the longest x1 1.29 us: body(): padded[:, LOW:LOW + HIGH] + from_low]
    ppermute x8, waiting for transfers between devices: 31 us -> 14.6 us  [the longest x1 8.53 us: body(): low = lax.ppermute(block[:, cells_y - LOW:], 'gy', forward_y)]
    unnamed x40 -> x42, local copies, waits for them, and re-layouts: 18.7 us -> 4.17 us
  transfers between devices with their start and end apart: 9 -> 9, of which waited for: 8 -> 5; matrix products, arithmetic and copies ran while one was open for 0% -> 2% of each run, Pallas kernels for 0% -> 0%
where the time goes in v1:
time: 843 us; the launch traced here: 828 us
  blocking collectives  471 us (56%)
  waiting for transfers between devices  107 us (13%)
  Pallas kernels  90.2 us (11%)
  local copies, waits for them, and re-layouts  73.4 us (9%)
  matrix products  54.1 us (6%)
  other arithmetic  16.8 us (2%)
  starting transfers between devices  16 us (2%)
    all_to_all x1, blocking collectives, body(): lax.all_to_all(turned, 'gy', split_axis=1, concat_axis=2, tiled=True)  188 us
    all_to_all x1, blocking collectives, body(): lax.all_to_all(slabs, 'gy', split_axis=2, concat_axis=1, tiled=True)  187 us
    all_to_all x1, blocking collectives, body(): lax.all_to_all(inverse, 'gx', split_axis=0, concat_axis=1, tiled=True)  95.9 us
    all_to_all x1, waiting for transfers between devices, body(): lax.all_to_all(pencils, 'gx', split_axis=1, concat_axis=0, tiled=True)  91.9 us
    pallas_call x1, Pallas kernels, body(): pl.pallas_call(functools.partial(spread_kernel, rows_y), out_shape=jax.Sh...  45.9 us
    pallas_call x1, Pallas kernels, body(): pl.pallas_call(functools.partial(sample_kernel, rows_y), out_shape=jax.Sh...  44.3 us
  transfers between devices with their start and end apart: 9, of which 5 were waited for; matrix products, arithmetic and copies ran while one was open for 2% of the time, Pallas kernels for 0%

profile of v1, /device:TPU:0, one launch (start us, length us, event | category | flops | bytes accessed | tf_op | source)
XLA Modules:
  0.0 828.4 jit_solution(13611866669183440660)
XLA Ops:
  0.0 1.1 slice_bitcast_fusion.2
  1.1 1.0 slice_bitcast_fusion
  2.1 0.9 copy-done
  3.0 0.9 copy-done.3
  3.9 0.7 copy-done.5
  5.2 45.9 %spread.1 = f32[131,72,256]{2,1,0:T(8,128)} custom-call(s32[256]{0:T(256)S(1)} %copy-done.5, s32[256]{0:T(256)S(1)} %copy-done.7, f32[256,128]{1,0:T(8,128)S(1)} %copy-done, f32[256,128]{1,0:T(8,128)S(1)} %get-tuple-element.6.fx, f32[256,128]{1,0:T(8,128)S(1)} %get-tuple-element.7.fy, f32[256,128]{1,0:T(8,128)S(1)} %get-tuple-element.5.fz, ...), custom_call_target="tpu_custom_call" | custom-call | flops 8858370048 | bytes 9658368 | tf_op jit(solution)/shard_map/spread/pallas_call | solution.py:170
  51.2 0.9 slice.80
  52.0 2.5 collective-permute-start.1
  54.5 0.9 slice.77
  55.5 4.2 slice.78
  59.8 0.9 slice_add_fusion.1
  60.7 0.9 slice_add_fusion
  61.6 0.8 pad_maximum_fusion.4
  62.4 0.7 pad_maximum_fusion.6
  63.2 1.5 collective-permute-start.2
  64.7 3.2 collective-permute-start.3
  67.9 1.5 pad_maximum_fusion
  69.5 4.8 slice.81
  74.3 2.1 collective-permute-done.3
  76.4 1.0 maximum_add_fusion.1
  77.5 1.3 maximum_add_fusion
  78.8 0.9 slice-done.1
  79.7 2.0 pad_maximum_fusion.1
  81.7 9.2 %fusion.12 = f32[128,256,64]{1,0,2:T(8,128)} fusion(f32[256,256,1]{1,0,2:T(8,128)S(1)} %copy-done.15, f32[128,64,256]{2,1,0:T(8,128)S(1)} %pad_maximum_fusion.1), kind=kOutput, calls=%fused_computation.15 | convolution fusion | flops 3221225472 | bytes 17039360 | tf_op jit(solution)/shard_map/xyz,zk->xky/dot_general | solution.py:210
  90.9 8.7 %copy.34 = f32[128,256,64]{0,2,1:T(8,128)} copy(f32[128,256,64]{1,0,2:T(8,128)} %fusion.12) | data formatting | bytes 16777216 | tf_op jit(solution)/shard_map/xyz,zk->xky/transpose | solution.py:210
  99.6 187.9 %all_to_all.72 = f32[128,256,64]{0,2,1:T(8,128)S(1)} all-to-all(f32[128,256,64]{0,2,1:T(8,128)} %copy.34), channel_id=1, replica_groups=mesh['gx'=4,'gy'=8] {'gy'}, dimensions={1} | all-to-all | bytes 16777216 | tf_op jit(solution)/shard_map/all_to_all | solution.py:211
  287.6 1.7 copy.35
  289.2 9.4 %fusion.16 = f32[128,32,512]{2,0,1:T(8,128)} fusion(f32[128,32,512]{0,2,1:T(8,128)S(1)} %bitcast.41, f32[512,512,1]{1,0,2:T(8,128)S(1)} %copy-done.11), kind=kOutput, calls=%fused_computation.33 | convolution fusion | flops 6442450944 | bytes 17825792 | tf_op jit(solution)/shard_map/xzy,yk->xzk/dot_general | solution.py:212
  298.6 5.8 all-to-all-start.1
  304.5 1.1 broadcast_add_fusion
  305.6 91.9 %all-to-all-done.1 = f32[128,32,512]{2,0,1:T(8,128)} async-done(((f32[128,32,512]{2,0,1:T(8,128)}), f32[128,32,512]{2,0,1:T(8,128)}, u32[]{:S(2)}, u32[]{:S(2)}) %all-to-all-start.1) | async-done | bytes 8388640 | tf_op jit(solution)/shard_map/all_to_all | solution.py:213
  397.6 8.2 copy.37
  405.8 11.5 %fusion = f32[512,8,512]{2,0,1:T(8,128)S(1)} fusion(f32[512,512,1]{0,1,2:T(8,128)S(1)} %copy-done.12, f32[512,8,512]{2,1,0:T(8,128)S(1)} %bitcast.38), kind=kOutput, calls=%fused_computation.3 | convolution fusion | flops 6442450944 | bytes 17825792 | tf_op jit(solution)/shard_map/xzy,xk->kzy/dot_general | solution.py:215
  417.3 8.2 fusion.4
  425.5 5.0 copy.40
  430.6 95.9 %all_to_all.73 = f32[512,8,512]{2,1,0:T(8,128)S(1)} all-to-all(f32[512,8,512]{2,1,0:T(8,128)S(1)} %copy.40), channel_id=1, replica_groups=mesh['gx'=4,'gy'=8] {'gx'}, dimensions={0} | all-to-all | bytes 16777216 | tf_op jit(solution)/shard_map/all_to_all | solution.py:220
  526.4 4.9 copy.41
  531.3 9.0 %fusion.17 = f32[128,32,512]{2,0,1:T(8,128)} fusion(f32[128,32,512]{2,0,1:T(8,128)S(1)} %bitcast.39, f32[512,512,1]{1,0,2:T(8,128)S(1)} %copy-done.11), kind=kOutput, calls=%fused_computation.34 | convolution fusion | flops 6442450944 | bytes 17825792 | tf_op jit(solution)/shard_map/xzy,yk->xzk/dot_general | solution.py:221
  540.3 10.3 %copy.42 = f32[128,32,512]{0,1,2:T(8,128)} copy(f32[128,32,512]{2,0,1:T(8,128)} %fusion.17) | data formatting | bytes 16777216 | tf_op jit(solution)/shard_map/xzy,yk->xzk/dot_general | solution.py:221
  550.6 187.0 %all_to_all.74 = f32[128,32,512]{0,1,2:T(8,128)S(1)} all-to-all(f32[128,32,512]{0,1,2:T(8,128)} %copy.42), channel_id=1, replica_groups=mesh['gx'=4,'gy'=8] {'gy'}, dimensions={2} | all-to-all | bytes 16777216 | tf_op jit(solution)/shard_map/all_to_all | solution.py:222
  737.5 8.1 copy.43
  745.7 9.3 %copy.50 = f32[128,256,64]{1,2,0:T(8,128)} copy(f32[128,256,64]{0,2,1:T(8,128)} %bitcast.43) | data formatting | bytes 16777216 | tf_op jit(solution)/shard_map/xzy,zk->xyk/dot_general | solution.py:223
  755.0 6.8 fusion.18
  762.4 3.9 collective-permute-done.4
  766.3 2.4 collective-permute-start.7
  769.0 8.5 %collective-permute-done.6 = f32[131,1,256]{2,1,0:T(1,128)S(1)} collective-permute-done((f32[131,1,256]{2,1,0:T(1,128)S(1)}, f32[131,1,256]{2,1,0:T(1,128)S(1)}, u32[]{:S(2)}, u32[]{:S(2)}) %collective-permute-start.6) | collective-permute-done | bytes 134176 | tf_op jit(solution)/shard_map/ppermute | solution.py:228
  777.7 6.2 maximum_maximum_fusion.field
  783.9 44.3 %sample.1 = f32[256,128]{1,0:T(8,128)} custom-call(s32[256]{0:T(256)S(1)} %copy-done.6, s32[256]{0:T(256)S(1)} %copy-done.8, f32[256,128]{1,0:T(8,128)S(1)} %copy-done.1, f32[256,128]{1,0:T(8,128)S(1)} %copy-done.2, f32[256,128]{1,0:T(8,128)S(1)} %get-tuple-element.6.fx, f32[256,128]{1,0:T(8,128)S(1)} %get-tuple-element.7.fy, ...), custom_call_target="tpu_custom_call" | custom-call | flops 8858370048 | bytes 9658368 | tf_op jit(solution)/shard_map/sample/pallas_call | solution.py:233
  (56 shorter events, 1.9 us)
Async XLA Ops:
  2.1 0.9 copy-start
  3.0 0.9 copy-start.3
  3.9 0.7 copy-start.5
  4.5 0.7 copy-start.7
  52.0 7.7 collective-permute-start.1
  55.5 5.2 collective-permute-start
  61.6 1.6 copy-start.9
  63.2 14.3 %collective-permute-start.2 = (f32[128,2,256]{2,1,0:T(2,128)}, f32[128,2,256]{2,1,0:T(2,128)}, u32[]{:S(2)}, u32[]{:S(2)}) collective-permute-start(f32[128,2,256]{2,1,0:T(2,128)} %pad_maximum_fusion.4), channel_id=1, source_target_pairs={{0,1},{1,2},{2,3},{3,4},{4,5},{5,6},{6,7},{7,0},{8,9},{9,10},{10,1... | collective-permute-start | bytes 786440 | tf_op jit(solution)/shard_map/ppermute | solution.py:192
  64.7 11.7 %collective-permute-start.3 = (f32[128,1,256]{2,1,0:T(1,128)}, f32[128,1,256]{2,1,0:T(1,128)}, u32[]{:S(2)}, u32[]{:S(2)}) collective-permute-start(f32[128,1,256]{2,1,0:T(1,128)} %pad_maximum_fusion.6), channel_id=1, source_target_pairs={{1,0},{2,1},{3,2},{4,3},{5,4},{6,5},{7,6},{0,7},{9,8},{10,9},{11,1... | collective-permute-start | bytes 393224 | tf_op jit(solution)/shard_map/ppermute | solution.py:195
  69.4 7.0 copy-start.10
  74.3 4.4 slice-start
  77.4 2.3 slice-start.1
  79.7 2.0 copy-start.15
  287.6 1.7 copy-start.11
  298.6 5.8 copy-start.18
  298.6 5.9 copy-start.17
  298.6 5.9 copy-start.16
  298.6 99.0 %all-to-all-start.1 = ((f32[128,32,512]{2,0,1:T(8,128)}), f32[128,32,512]{2,0,1:T(8,128)}, u32[]{:S(2)}, u32[]{:S(2)}) async-start(f32[128,32,512]{2,0,1:T(8,128)} %fusion.16), calls=%async_computation.1 | async-start | bytes 16777216 | tf_op jit(solution)/shard_map/all_to_all | solution.py:213
  305.6 100.2 %copy-start.12 = (f32[512,512,1]{0,1,2:T(8,128)S(1)}, f32[512,512,1]{0,1,2:T(8,128)}, u32[]{:S(2)}) copy-start(f32[512,512,1]{0,1,2:T(8,128)} %constant.35) | copy-start | bytes 3145732
  405.8 11.5 %copy-start.13 = (f32[512,512]{1,0:T(8,128)S(1)}, f32[512,512]{1,0:T(8,128)}, u32[]{:S(2)}) copy-start(f32[512,512]{1,0:T(8,128)} %broadcast_add_fusion) | copy-start | bytes 3145732
  745.7 9.3 %copy-start.14 = (f32[256,256,1]{1,0,2:T(8,128)S(1)}, f32[256,256,1]{1,0,2:T(8,128)}, u32[]{:S(2)}) copy-start(f32[256,256,1]{1,0,2:T(8,128)} %constant.37) | copy-start | bytes 786436
  761.8 4.4 collective-permute-start.5
  761.9 4.4 collective-permute-start.4
  766.3 11.3 %collective-permute-start.7 = (f32[131,2,256]{2,1,0:T(2,128)S(1)}, f32[131,2,256]{2,1,0:T(2,128)S(1)}, u32[]{:S(2)}, u32[]{:S(2)}) collective-permute-start(f32[131,2,256]{2,1,0:T(2,128)S(1)} %pad_maximum_fusion.2), channel_id=1, source_target_pairs={{1,0},{2,1},{3,2},{4,3},{5,4},{6,5},{7,6},{0,7},{9,8},{10,9},{11,1... | collective-permute-start | bytes 804872 | tf_op jit(solution)/shard_map/ppermute | solution.py:229
  768.9 8.7 %collective-permute-start.6 = (f32[131,1,256]{2,1,0:T(1,128)S(1)}, f32[131,1,256]{2,1,0:T(1,128)S(1)}, u32[]{:S(2)}, u32[]{:S(2)}) collective-permute-start(f32[131,1,256]{2,1,0:T(1,128)S(1)} %pad_maximum_fusion.5), channel_id=1, source_target_pairs={{0,1},{1,2},{2,3},{3,4},{4,5},{5,6},{6,7},{7,0},{8,9},{9,10},{10,1... | collective-permute-start | bytes 402440 | tf_op jit(solution)/shard_map/ppermute | solution.py:228
  769.0 14.8 %copy-start.1 = (f32[256,128]{1,0:T(8,128)S(1)}, f32[256,128]{1,0:T(8,128)}, u32[]{:S(2)}) copy-start(f32[256,128]{1,0:T(8,128)} %values.3) | copy-start | bytes 393220
  769.0 14.8 %copy-start.2 = (f32[256,128]{1,0:T(8,128)S(1)}, f32[256,128]{1,0:T(8,128)}, u32[]{:S(2)}) copy-start(f32[256,128]{1,0:T(8,128)} %noise.1) | copy-start | bytes 393220
  769.0 14.8 %copy-start.4 = (s32[256,128]{1,0:T(8,128)S(1)}, s32[256,128]{1,0:T(8,128)}, u32[]{:S(2)}) copy-start(s32[256,128]{1,0:T(8,128)} %cz.3) | copy-start | bytes 393220
  769.0 14.8 %copy-start.6 = (s32[256]{0:T(256)S(1)}, s32[256]{0:T(256)}, u32[]{:S(2)}) copy-start(s32[256]{0:T(256)} %tile_grid.3) | copy-start | bytes 3076
  769.0 14.8 %copy-start.8 = (s32[256]{0:T(256)S(1)}, s32[256]{0:T(256)}, u32[]{:S(2)}) copy-start(s32[256]{0:T(256)} %counts.3) | copy-start | bytes 3076

commit v2 on v1

--- a/solution.py
+++ b/solution.py
@@ -93,16 +93,16 @@
         boxes = []
         for row in range(GROUP):
             source = jnp.where(slot < counts[first + row], value[row : row + 1], 0.0)
-            wide_x = box_weights(taps_x, c0, row) * source
-            wide_y = box_weights(taps_y, c1, row)
-            plane = jnp.concatenate([wide_x[x : x + 1] * wide_y for x in range(SIDE)], 0)
+            wide_x = box_weights(taps_x, c0, row)
+            wide_y = box_weights(taps_y, c1, row) * source
+            plane = jnp.concatenate([wide_y[y : y + 1] * wide_x for y in range(SIDE)], 0)
             column = column_weights(taps_z, c2, row, depth)
             boxes.append(split_dot(plane, column, ((1,), (1,))))
         for row in range(GROUP):
             owner = tile_grid[first + row]
-            at_x = (owner // rows_y) * TILE
-            at_y = pl.multiple_of(lax.rem(owner, rows_y) * TILE, TILE)
-            padded[pl.ds(at_x, SIDE), pl.ds(at_y, WINDOW), :] += boxes[row].reshape(
+            at_x = pl.multiple_of((owner // rows_y) * TILE, TILE)
+            at_y = lax.rem(owner, rows_y) * TILE
+            padded[pl.ds(at_y, SIDE), pl.ds(at_x, WINDOW), :] += boxes[row].reshape(
                 SIDE, WINDOW, depth
             )
         return carry
@@ -126,23 +126,292 @@
         rows = []
         for row in range(GROUP):
             owner = tile_grid[first + row]
-            at_x = (owner // rows_y) * TILE
-            at_y = pl.multiple_of(lax.rem(owner, rows_y) * TILE, TILE)
-            box = field[pl.ds(at_x, SIDE), pl.ds(at_y, WINDOW), :].reshape(SIDE * WINDOW, depth)
+            at_x = pl.multiple_of((owner // rows_y) * TILE, TILE)
+            at_y = lax.rem(owner, rows_y) * TILE
+            box = field[pl.ds(at_y, SIDE), pl.ds(at_x, WINDOW), :].reshape(SIDE * WINDOW, depth)
             column = column_weights(taps_z, c2, row, depth)
             along = split_dot(box, column, ((1,), (0,))).reshape(SIDE, WINDOW, points)
             wide_x = box_weights(taps_x, c0, row)
             wide_y = box_weights(taps_y, c1, row)
-            total = along[0] * wide_x[0:1]
-            for x in range(1, SIDE):
-                total = total + along[x] * wide_x[x : x + 1]
-            sampled = jnp.sum(total * wide_y, axis=0, keepdims=True)
+            total = along[0] * wide_y[0:1]
+            for y in range(1, SIDE):
+                total = total + along[y] * wide_y[y : y + 1]
+            sampled = jnp.sum(total * wide_x, axis=0, keepdims=True)
             result = level[row : row + 1] * value[row : row + 1] + sampled
             rows.append(jnp.where(slot < counts[first + row], result, 0.0))
         product[pl.ds(first, GROUP), :] = jnp.concatenate(rows, 0)
         return carry
 
     lax.fori_loop(0, values.shape[0] // GROUP, step, 0)
+
+
+def remote(source, target, send, recv, axis, peer):
+    return pltpu.make_async_remote_copy(
+        src_ref=source,
+        dst_ref=target,
+        send_sem=send,
+        recv_sem=recv,
+        device_id={axis: peer},
+        device_id_type=pl.DeviceIdType.MESH,
+    )
+
+
+def planes_kernel(
+    ranks_x,
+    ranks_y,
+    chunks,
+    scale,
+    rate_z,
+    rate_x,
+    rate_y,
+    x_top,
+    x_rest,
+    y_top,
+    y_rest,
+    turned,
+    returned,
+    pencils,
+    outgoing,
+    planes,
+    slabs,
+    y_send,
+    y_recv,
+    x_send,
+    x_recv,
+    back_x_send,
+    back_x_recv,
+    back_y_send,
+    back_y_recv,
+    local,
+):
+    me_x, me_y = lax.axis_index("gx"), lax.axis_index("gy")
+    group = planes.shape[2]
+    cells_x = planes.shape[4]
+    cells_y = turned.shape[1]
+    per_chunk = ranks_x * group
+    per_rank = chunks * per_chunk
+    peers_x = [lax.rem(me_x + step, ranks_x) for step in range(1, ranks_x)]
+    peers_y = [lax.rem(me_y + step, ranks_y) for step in range(1, ranks_y)]
+
+    barrier = pltpu.get_barrier_semaphore()
+    for axis, peers in (("gx", peers_x), ("gy", peers_y)):
+        for peer in peers:
+            pl.semaphore_signal(
+                barrier, inc=1, device_id={axis: peer}, device_id_type=pl.DeviceIdType.MESH
+            )
+    pl.semaphore_wait(barrier, ranks_x + ranks_y - 2)
+
+    def planes_of(ref, rank, chunk):
+        return ref.at[pl.ds(rank * per_rank + chunk * per_chunk, per_chunk)]
+
+    def rows_of(chunk, rank):
+        return pencils.at[chunk, :, pl.ds(pl.multiple_of(rank * cells_y, cells_y), cells_y)]
+
+    def forward_y(chunk, peer):
+        return remote(
+            planes_of(turned, peer, chunk), rows_of(chunk, me_y),
+            y_send.at[chunk, peer], y_recv.at[chunk, me_y], "gy", peer,
+        )
+
+    def arrived_y(chunk, peer):
+        return remote(
+            planes_of(turned, peer, chunk), rows_of(chunk, peer),
+            y_send.at[chunk, peer], y_recv.at[chunk, peer], "gy", peer,
+        )
+
+    def own_y(chunk):
+        return pltpu.make_async_copy(
+            planes_of(turned, me_y, chunk), rows_of(chunk, me_y), local.at[0, chunk]
+        )
+
+    def forward_x(chunk, peer, slot):
+        return remote(
+            outgoing.at[chunk, peer], planes.at[chunk, slot],
+            x_send.at[chunk, peer], x_recv.at[chunk, slot], "gx", peer,
+        )
+
+    def own_x(chunk):
+        return pltpu.make_async_copy(
+            outgoing.at[chunk, me_x], planes.at[chunk, me_x], local.at[1, chunk]
+        )
+
+    def back_x(chunk, peer, slot):
+        return remote(
+            planes.at[chunk, peer], slabs.at[chunk, slot],
+            back_x_send.at[chunk, peer], back_x_recv.at[chunk, slot], "gx", peer,
+        )
+
+    def own_back_x(chunk):
+        return pltpu.make_async_copy(
+            planes.at[chunk, me_x], slabs.at[chunk, me_x], local.at[2, chunk]
+        )
+
+    def back_y(chunk, peer, slot):
+        return remote(
+            rows_of(chunk, peer), planes_of(returned, slot, chunk),
+            back_y_send.at[chunk, peer], back_y_recv.at[chunk, slot], "gy", peer,
+        )
+
+    def own_back_y(chunk):
+        return pltpu.make_async_copy(
+            rows_of(chunk, me_y), planes_of(returned, me_y, chunk), local.at[3, chunk]
+        )
+
+    def table_dot(top, rest, right):
+        right_top, right_rest = halves(right)
+
+        def dot(a, b):
+            return jnp.dot(a, b, preferred_element_type=jnp.float32)
+
+        return dot(top, right_top) + (dot(top, right_rest) + dot(rest, right_top))
+
+    def dot_table(left, top, rest):
+        left_top, left_rest = halves(left)
+
+        def dot(a, b):
+            return jnp.dot(a, b, preferred_element_type=jnp.float32)
+
+        return dot(left_top, top) + (dot(left_top, rest) + dot(left_rest, top))
+
+    def send(chunk):
+        own_y(chunk).start()
+        for peer in peers_y:
+            forward_y(chunk, peer).start()
+
+    def along_y(chunk):
+        own_y(chunk).wait()
+        for peer in peers_y:
+            arrived_y(chunk, peer).wait_recv()
+
+        def one(index, carry):
+            owner, plane = index // group, lax.rem(index, group)
+            outgoing[chunk, owner, plane] = table_dot(
+                y_top[...], y_rest[...], pencils[chunk, index]
+            )
+            return carry
+
+        lax.fori_loop(0, per_chunk, one, 0)
+        own_x(chunk).start()
+        for peer in peers_x:
+            forward_x(chunk, peer, me_x).start()
+
+    def along_x(chunk):
+        own_x(chunk).wait()
+        for peer in peers_x:
+            forward_x(chunk, peer, peer).wait_recv()
+
+        def one(plane, carry):
+            whole = jnp.concatenate(
+                [planes[chunk, rank, plane] for rank in range(ranks_x)], 1
+            )
+            coeffs = dot_table(whole, x_top[...], x_rest[...])
+            at_z = me_y * per_rank + chunk * per_chunk + me_x * group + plane
+            denom = 1.0 + rate_x[...] + rate_y[...] + rate_z[at_z]
+            weighted = coeffs * (scale / (denom * denom))
+            inverse = dot_table(weighted, x_top[...], x_rest[...])
+            for rank in range(ranks_x):
+                planes[chunk, rank, plane] = inverse[:, rank * cells_x : (rank + 1) * cells_x]
+            return carry
+
+        lax.fori_loop(0, group, one, 0)
+        own_back_x(chunk).start()
+        for peer in peers_x:
+            back_x(chunk, peer, me_x).start()
+
+    def back_along_y(chunk):
+        own_back_x(chunk).wait()
+        for peer in peers_x:
+            back_x(chunk, peer, peer).wait_recv()
+
+        def one(index, carry):
+            owner, plane = index // group, lax.rem(index, group)
+            pencils[chunk, index] = table_dot(y_top[...], y_rest[...], slabs[chunk, owner, plane])
+            return carry
+
+        lax.fori_loop(0, per_chunk, one, 0)
+        own_back_y(chunk).start()
+        for peer in peers_y:
+            back_y(chunk, peer, me_y).start()
+
+    ahead = min(2, chunks)
+    for chunk in range(ahead):
+        send(chunk)
+
+    def step(index, carry):
+        @pl.when(index < chunks)
+        def _():
+            along_y(index)
+            for peer in peers_y:
+                forward_y(index, peer).wait_send()
+
+        @pl.when(index + ahead < chunks)
+        def _():
+            send(index + ahead)
+
+        @pl.when((index >= 1) & (index <= chunks))
+        def _():
+            along_x(index - 1)
+
+        @pl.when(index >= 2)
+        def _():
+            back_along_y(index - 2)
+
+        return carry
+
+    lax.fori_loop(0, chunks + 2, step, 0)
+
+    def finish(chunk, carry):
+        own_back_y(chunk).wait()
+        for peer in peers_x:
+            forward_x(chunk, peer, me_x).wait_send()
+            back_x(chunk, peer, me_x).wait_send()
+        for peer in peers_y:
+            back_y(chunk, peer, me_y).wait_send()
+            back_y(chunk, peer, peer).wait_recv()
+        return carry
+
+    lax.fori_loop(0, chunks, finish, 0)
+
+
+def smooth_planes(turned, rate_x, rate_y, rate_z, ranks_x, ranks_y):
+    depth, cells_y, cells_x = turned.shape
+    full_x, full_y = rate_x.shape[0], rate_y.shape[0]
+    planes_dev = depth // (ranks_x * ranks_y)
+    chunks = math.gcd(planes_dev, 4)
+    group = planes_dev // chunks
+    x_top, x_rest = halves(cas_table(full_x))
+    y_top, y_rest = halves(cas_table(full_y))
+    vmem = pl.BlockSpec(memory_space=pltpu.VMEM)
+    anywhere = pl.BlockSpec(memory_space=pl.ANY)
+    block = (chunks, ranks_x, group, full_y, cells_x)
+    sems_x = pltpu.SemaphoreType.DMA((chunks, ranks_x))
+    sems_y = pltpu.SemaphoreType.DMA((chunks, ranks_y))
+    flops = 6 * 2 * turned.size * (full_x + full_y) * 2
+    return pl.pallas_call(
+        functools.partial(
+            planes_kernel, ranks_x, ranks_y, chunks, 4.0 / (full_x * full_y * depth)
+        ),
+        out_shape=jax.ShapeDtypeStruct(turned.shape, jnp.float32),
+        in_specs=[pl.BlockSpec(memory_space=pltpu.SMEM)] + [vmem] * 6 + [anywhere],
+        out_specs=anywhere,
+        scratch_shapes=[
+            pltpu.VMEM((chunks, ranks_x * group, full_y, cells_x), jnp.float32),
+            pltpu.VMEM(block, jnp.float32),
+            pltpu.VMEM(block, jnp.float32),
+            pltpu.VMEM(block, jnp.float32),
+            sems_y, sems_y, sems_x, sems_x, sems_x, sems_x, sems_y, sems_y,
+            pltpu.SemaphoreType.DMA((4, chunks)),
+        ],
+        compiler_params=pltpu.CompilerParams(
+            collective_id=0, has_side_effects=True, vmem_limit_bytes=VMEM_BYTES
+        ),
+        cost_estimate=pl.CostEstimate(
+            flops=flops, bytes_accessed=8 * turned.size, transcendentals=0
+        ),
+        name="smooth",
+    )(
+        rate_z, rate_x[None, :], rate_y[:, None], x_top, x_rest, y_top, y_rest, turned
+    )
 
 
 def body(values, noise, fractions, cell_xy, cell_z, tile_grid, counts, rate_x, rate_y, rate_z):
@@ -155,8 +424,8 @@
     cells_x = full_x // ranks_x
     cells_y = full_y // ranks_y
     rows_y = cells_y // TILE
-    wide_x = cells_x + LOW + HIGH
-    wide_y = cells_y + TILE
+    wide_x = cells_x + TILE
+    wide_y = cells_y + LOW + HIGH
     smem = pl.BlockSpec(memory_space=pltpu.SMEM)
     vmem = pl.BlockSpec(memory_space=pltpu.VMEM)
     params = pltpu.CompilerParams(vmem_limit_bytes=VMEM_BYTES)
@@ -169,7 +438,7 @@
     )
     padded = pl.pallas_call(
         functools.partial(spread_kernel, rows_y),
-        out_shape=jax.ShapeDtypeStruct((wide_x, wide_y, depth), jnp.float32),
+        out_shape=jax.ShapeDtypeStruct((wide_y, wide_x, depth), jnp.float32),
         in_specs=[smem, smem] + [vmem] * 7,
         out_specs=vmem,
         compiler_params=params,
@@ -179,55 +448,41 @@
 
     forward_x, backward_x = ring("gx")
     forward_y, backward_y = ring("gy")
-    from_low = lax.ppermute(padded[cells_x + LOW :], "gx", forward_x)
-    from_high = lax.ppermute(padded[:LOW], "gx", backward_x)
+    from_low = lax.ppermute(padded[cells_y + LOW :], "gy", forward_y)
+    from_high = lax.ppermute(padded[:LOW], "gy", backward_y)
     padded = jnp.concatenate(
         [
             padded[LOW : LOW + HIGH] + from_low,
-            padded[LOW + HIGH : cells_x],
-            padded[cells_x : cells_x + LOW] + from_high,
+            padded[LOW + HIGH : cells_y],
+            padded[cells_y : cells_y + LOW] + from_high,
         ],
         0,
     )
     from_low = lax.ppermute(
-        padded[:, cells_y + LOW : cells_y + LOW + HIGH], "gy", forward_y
-    )
-    from_high = lax.ppermute(padded[:, :LOW], "gy", backward_y)
+        padded[:, cells_x + LOW : cells_x + LOW + HIGH], "gx", forward_x
+    )
+    from_high = lax.ppermute(padded[:, :LOW], "gx", backward_x)
     spread_grid = jnp.concatenate(
         [
             padded[:, LOW : LOW + HIGH] + from_low,
-            padded[:, LOW + HIGH : cells_y],
-            padded[:, cells_y : cells_y + LOW] + from_high,
+            padded[:, LOW + HIGH : cells_x],
+            padded[:, cells_x : cells_x + LOW] + from_high,
         ],
         1,
     )
 
-    table_x = cas_table(full_x)
-    table_y = cas_table(full_y)
     table_z = cas_table(depth)
-    planes_dev = depth // (ranks_x * ranks_y)
     einsum = functools.partial(jnp.einsum, precision=lax.Precision.HIGH)
-    turned = einsum("xyz,zk->xky", spread_grid, table_z)
-    pencils = lax.all_to_all(turned, "gy", split_axis=1, concat_axis=2, tiled=True)
-    pencils = einsum("xzy,yk->xzk", pencils, table_y)
-    planes = lax.all_to_all(pencils, "gx", split_axis=1, concat_axis=0, tiled=True)
-    z_start = lax.axis_index("gy") * (depth // ranks_y) + lax.axis_index("gx") * planes_dev
-    planes = einsum("xzy,xk->kzy", planes, table_x)
-    local_rate = lax.dynamic_slice_in_dim(rate_z, z_start, planes_dev)
-    denom = 1.0 + rate_x[:, None, None] + rate_y[None, None, :] + local_rate[None, :, None]
-    weighted = planes * ((4.0 / (full_x * full_y * depth)) / (denom * denom))
-    inverse = einsum("kzy,kx->xzy", weighted, table_x)
-    slabs = lax.all_to_all(inverse, "gx", split_axis=0, concat_axis=1, tiled=True)
-    slabs = einsum("xzy,yk->xzk", slabs, table_y)
-    returned = lax.all_to_all(slabs, "gy", split_axis=2, concat_axis=1, tiled=True)
-    block = einsum("xzy,zk->xyk", returned, table_z)
-
-    low = lax.ppermute(block[cells_x - LOW :], "gx", forward_x)
-    high = lax.ppermute(block[:HIGH], "gx", backward_x)
+    turned = einsum("kz,yxz->kyx", table_z, spread_grid)
+    returned = smooth_planes(turned, rate_x, rate_y, rate_z, ranks_x, ranks_y)
+    block = einsum("kyx,kz->yxz", returned, table_z)
+
+    low = lax.ppermute(block[cells_y - LOW :], "gy", forward_y)
+    high = lax.ppermute(block[:HIGH], "gy", backward_y)
     block = jnp.concatenate([low, block, high], 0)
-    low = lax.ppermute(block[:, cells_y - LOW :], "gy", forward_y)
-    high = lax.ppermute(block[:, :HIGH], "gy", backward_y)
-    spare = jnp.zeros((wide_x, TILE - LOW - HIGH, depth), jnp.float32)
+    low = lax.ppermute(block[:, cells_x - LOW :], "gx", forward_x)
+    high = lax.ppermute(block[:, :HIGH], "gx", backward_x)
+    spare = jnp.zeros((wide_y, TILE - LOW - HIGH, depth), jnp.float32)
     field = jnp.concatenate([low, block, high, spare], 1)
 
     return pl.pallas_call(

time: 843 us -> 545 us (0.65); the launches traced: 828 us -> 544 us
  blocking collectives: 471 us -> 0 us
  Pallas kernels: 90.2 us -> 445 us
  waiting for transfers between devices: 107 us -> 14.1 us
  local copies, waits for them, and re-layouts: 73.4 us -> 30.8 us
  matrix products: 54.1 us -> 18.5 us
  starting transfers between devices: 16 us -> 26.2 us
    all_to_all x3 -> x0, blocking collectives: 471 us -> none  [the longest x1 188 us: body(): lax.all_to_all(turned, 'gy', split_axis=1, concat_axis=2, tiled=True)]
    pallas_call x0 -> x1, Pallas kernels: none -> 356 us  [smooth_planes(): pl.pallas_call(functools.partial(planes_kernel, ranks_x, ranks_y, chunks,...]
    all_to_all x1 -> x0, waiting for transfers between devices: 91.9 us -> none  [body(): lax.all_to_all(pencils, 'gx', split_axis=1, concat_axis=0, tiled=True)]
    dot_general x6 -> x2, matrix products: 54.1 us -> 18.5 us  [the longest x1 13.7 us: body(): block = einsum('kyx,kz->yxz', returned, table_z)]
    all_to_all x4 -> x0, local copies, waits for them, and re-layouts: 22.9 us -> none  [the longest x1 8.24 us: body(): lax.all_to_all(pencils, 'gx', split_axis=1, concat_axis=0, tiled=True)]
    dot_general x3 -> x1, local copies, waits for them, and re-layouts: 24.6 us -> 8.13 us  [body(): turned = einsum('kz,yxz->kyx', table_z, spread_grid)]
    ppermute x8, starting transfers between devices: 10.3 us -> 26.2 us  [the longest x1 18.6 us: body(): high = lax.ppermute(block[:HIGH], 'gy', backward_y)]
    transpose x1 -> x0, local copies, waits for them, and re-layouts: 8.71 us -> none  [body(): turned = einsum('xyz,zk->xky', spread_grid, table_z)]
  transfers between devices with their start and end apart: 9 -> 8, of which waited for: 5 -> 3; matrix products, arithmetic and copies ran while one was open for 2% -> 3% of each run, Pallas kernels for 0% -> 0%
where the time goes in v2:
time: 545 us; the launch traced here: 544 us
  Pallas kernels  445 us (82%)
  local copies, waits for them, and re-layouts  30.8 us (6%)
  starting transfers between devices  26.2 us (5%)
  matrix products  18.5 us (3%)
  waiting for transfers between devices  14.1 us (3%)
  other arithmetic  8.71 us (2%)
    pallas_call x1, Pallas kernels, smooth_planes(): pl.pallas_call(functools.partial(planes_kernel, ranks_x, ranks_y, chunks,...  356 us
    pallas_call x1, Pallas kernels, body(): pl.pallas_call(functools.partial(spread_kernel, rows_y), out_shape=jax.Sh...  44.9 us
    pallas_call x1, Pallas kernels, body(): pl.pallas_call(functools.partial(sample_kernel, rows_y), out_shape=jax.Sh...  44.4 us
    ppermute x1, starting transfers between devices, body(): high = lax.ppermute(block[:HIGH], 'gy', backward_y)  18.6 us
    dot_general x1, matrix products, body(): block = einsum('kyx,kz->yxz', returned, table_z)  13.7 us
  transfers between devices with their start and end apart: 8, of which 3 were waited for; matrix products, arithmetic and copies ran while one was open for 3% of the time, Pallas kernels for 0%

profile of v2, /device:TPU:0, one launch (start us, length us, event | category | flops | bytes accessed | tf_op | source)
XLA Modules:
  0.0 543.8 jit_solution(2037257525168879295)
XLA Ops:
  0.0 1.0 slice_bitcast_fusion
  1.0 1.1 slice_bitcast_fusion.2
  2.1 0.0 copy-start
  2.1 0.9 copy-done
  3.0 0.9 copy-done.3
  3.9 0.7 copy-done.7
  4.5 0.7 copy-done.9
  5.2 44.9 %spread.1 = f32[67,136,256]{2,1,0:T(8,128)} custom-call(s32[256]{0:T(256)S(1)} %copy-done.7, s32[256]{0:T(256)S(1)} %copy-done.9, f32[256,128]{1,0:T(8,128)S(1)} %copy-done, f32[256,128]{1,0:T(8,128)S(1)} %get-tuple-element.6.fx, f32[256,128]{1,0:T(8,128)S(1)} %get-tuple-element.7.fy, f32[256,128]{1,0:T(8,128)S(1)} %get-tuple-element.5.fz, ...), custom_call_target="tpu_custom_call" | custom-call | flops 8858370048 | bytes 9330688 | tf_op jit(solution)/shard_map/spread/pallas_call | solution.py:439
  50.1 0.9 slice.80
  51.0 6.0 %collective-permute-start.1 = (f32[1,136,256]{2,1,0:T(8,128)S(1)}, f32[1,136,256]{2,1,0:T(8,128)S(1)}, u32[]{:S(2)}, u32[]{:S(2)}) collective-permute-start(f32[1,136,256]{2,1,0:T(8,128)S(1)} %slice.80), channel_id=1, source_target_pairs={{1,0},{2,1},{3,2},{4,3},{5,4},{6,5},{7,6},{0,7},{9,8},{10,9},{11,1... | collective-permute-start | bytes 417800 | tf_op jit(solution)/shard_map/ppermute | solution.py:452
  57.0 1.0 slice.77
  58.0 0.0 copy-start.15
  58.0 0.1 collective-permute-start
  58.1 7.3 %slice.78 = f32[61,136,256]{2,1,0:T(8,128)} slice(f32[67,136,256]{2,1,0:T(8,128)} %spread.1), slice={[3:64], [0:136], [0:256]} | slice | bytes 16990208 | tf_op jit(solution)/shard_map/slice | solution.py:456
  65.4 0.1 copy.15.rate_y
  65.6 1.1 slice_add_fusion.1
  66.7 2.3 collective-permute-done
  68.9 1.0 slice_add_fusion
  69.9 1.1 pad_maximum_fusion.5
  71.0 0.7 pad_maximum_fusion
  71.7 0.1 collective-permute-start.3
  71.7 0.1 pad_maximum_fusion.3
  71.8 0.7 collective-permute-start.2
  72.5 4.6 slice.81
  77.1 0.1 maximum_add_fusion.1
  77.2 0.0 slice-start.1
  77.2 0.1 maximum_add_fusion
  77.3 2.0 slice-done
  79.3 0.0 copy-done.14
  79.3 1.4 slice-done.1
  80.7 4.7 fusion
  85.4 0.0 copy-start.5
  85.4 0.0 copy-start.6
  85.4 0.0 copy-start.11
  85.5 0.0 copy-start.12
  85.5 8.1 %copy.17.turned = f32[256,64,128]{2,1,0:T(8,128)} copy(f32[256,64,128]{2,0,1:T(8,128)S(1)} %fusion) | data formatting | bytes 16777216 | tf_op jit(solution)/shard_map/kz,yxz->kyx/dot_general | solution.py:476
  93.6 356.0 %smooth.1 = f32[256,64,128]{2,1,0:T(8,128)} custom-call(f32[256]{0:T(256)S(1)} %copy-done.6, f32[1,512]{1,0:T(1,128)S(1)} %bitcast.15, f32[512,1]{1,0:T(8,128)S(1)} %copy.15.rate_y, bf16[512,512]{1,0:T(8,128)(2,1)S(1)} %copy-done.12, bf16[512,512]{1,0:T(8,128)(2,1)S(1)} %copy-done.11, bf16[512,512]{1,0:T(8,128)(2,1)S(1)} %copy-done.12, ...), custom_call_target="tpu_custom_call" | custom-call | flops 51539607552 | bytes 16777216 | tf_op jit(solution)/shard_map/smooth/pallas_call | solution.py:390
  449.7 13.7 %fusion.6 = f32[64,128,256]{2,1,0:T(8,128)S(1)} fusion(f32[256,256,1]{1,0,2:T(8,128)S(1)} %copy-done.14, f32[256,64,128]{2,1,0:T(8,128)} %smooth.1), kind=kOutput, calls=%fused_computation.8 | convolution fusion | flops 3221225472 | bytes 17039360 | tf_op jit(solution)/shard_map/kyx,kz->yxz/dot_general | solution.py:478
  463.4 18.6 %collective-permute-start.5 = (f32[2,128,256]{2,1,0:T(8,128)S(1)}, f32[2,128,256]{2,1,0:T(8,128)S(1)}, u32[]{:S(2)}, u32[]{:S(2)}) collective-permute-start(f32[2,128,256]{2,1,0:T(8,128)S(1)} %slice.83), channel_id=1, source_target_pairs={{1,0},{2,1},{3,2},{4,3},{5,4},{6,5},{7,6},{0,7},{9,8},{10,9},{11,1... | collective-permute-start | bytes 786440 | tf_op jit(solution)/shard_map/ppermute | solution.py:481
  482.1 0.1 collective-permute-start.4
  482.2 7.9 %collective-permute-done.4 = f32[1,128,256]{2,1,0:T(8,128)S(1)} collective-permute-done((f32[1,128,256]{2,1,0:T(8,128)S(1)}, f32[1,128,256]{2,1,0:T(8,128)S(1)}, u32[]{:S(2)}, u32[]{:S(2)}) %collective-permute-start.4) | collective-permute-done | bytes 131104 | tf_op jit(solution)/shard_map/ppermute | solution.py:480
  490.1 0.1 collective-permute-start.7
  490.2 0.1 pad_maximum_fusion.4
  490.3 0.5 collective-permute-start.6
  490.8 0.1 pad.5.clone
  490.9 3.9 collective-permute-done.6
  494.8 4.6 maximum_maximum_fusion.field
  499.4 44.4 %sample.1 = f32[256,128]{1,0:T(8,128)} custom-call(s32[256]{0:T(256)S(1)} %copy-done.8, s32[256]{0:T(256)S(1)} %copy-done.10, f32[256,128]{1,0:T(8,128)S(1)} %copy-done.1, f32[256,128]{1,0:T(8,128)S(1)} %copy-done.2, f32[256,128]{1,0:T(8,128)S(1)} %get-tuple-element.6.fx, f32[256,128]{1,0:T(8,128)S(1)} %get-tuple-element.7.fy, ...), custom_call_target="tpu_custom_call" | custom-call | flops 8858370048 | bytes 9330688 | tf_op jit(solution)/shard_map/sample/pallas_call | solution.py:488
  (32 shorter events, 0.1 us)
Async XLA Ops:
  2.1 0.9 copy-start
  3.0 0.9 copy-start.3
  3.9 0.7 copy-start.7
  4.5 0.7 copy-start.9
  51.0 14.6 %collective-permute-start.1 = (f32[1,136,256]{2,1,0:T(8,128)S(1)}, f32[1,136,256]{2,1,0:T(8,128)S(1)}, u32[]{:S(2)}, u32[]{:S(2)}) collective-permute-start(f32[1,136,256]{2,1,0:T(8,128)S(1)} %slice.80), channel_id=1, source_target_pairs={{1,0},{2,1},{3,2},{4,3},{5,4},{6,5},{7,6},{0,7},{9,8},{10,9},{11,1... | collective-permute-start | bytes 417800 | tf_op jit(solution)/shard_map/ppermute | solution.py:452
  58.0 7.4 %copy-start.15 = (f32[512]{0:T(512)S(1)}, f32[512]{0:T(512)}, u32[]{:S(2)}) copy-start(f32[512]{0:T(512)} %param.21) | copy-start | bytes 6148
  58.0 10.9 %collective-permute-start = (f32[2,136,256]{2,1,0:T(8,128)S(1)}, f32[2,136,256]{2,1,0:T(8,128)S(1)}, u32[]{:S(2)}, u32[]{:S(2)}) collective-permute-start(f32[2,136,256]{2,1,0:T(8,128)S(1)} %slice.77), channel_id=1, source_target_pairs={{0,1},{1,2},{2,3},{3,4},{4,5},{5,6},{6,7},{7,0},{8,9},{9,10},{10,1... | collective-permute-start | bytes 835592 | tf_op jit(solution)/shard_map/ppermute | solution.py:451
  65.6 5.4 copy-start.13
  71.7 5.5 %collective-permute-start.3 = (f32[64,1,256]{2,1,0:T(1,128)S(1)}, f32[64,1,256]{2,1,0:T(1,128)S(1)}, u32[]{:S(2)}, u32[]{:S(2)}) collective-permute-start(f32[64,1,256]{2,1,0:T(1,128)S(1)} %pad_maximum_fusion.5), channel_id=1, source_target_pairs={{8,0},{16,8},{24,16},{0,24},{9,1},{17,9},{25,17},{1,25},{10,2},{18... | collective-permute-start | bytes 196616 | tf_op jit(solution)/shard_map/ppermute | solution.py:464
  71.8 5.4 collective-permute-start.2
  77.1 2.2 slice-start
  77.1 2.2 copy-start.14
  77.2 3.5 slice-start.1
  85.4 8.2 %copy-start.5 = (f32[512]{0:T(512)S(1)}, f32[512]{0:T(512)}, u32[]{:S(2)}) copy-start(f32[512]{0:T(512)} %param.20) | copy-start | bytes 6148
  85.4 8.2 %copy-start.6 = (f32[256]{0:T(256)S(1)}, f32[256]{0:T(256)}, u32[]{:S(2)}) copy-start(f32[256]{0:T(256)} %rate_z.1) | copy-start | bytes 3076
  85.4 8.2 %copy-start.11 = (bf16[512,512]{1,0:T(8,128)(2,1)S(1)}, bf16[512,512]{1,0:T(8,128)(2,1)}, u32[]{:S(2)}) copy-start(bf16[512,512]{1,0:T(8,128)(2,1)} %constant.11.x_rest.y_rest) | copy-start | bytes 1572868
  85.5 8.2 %copy-start.12 = (bf16[512,512]{1,0:T(8,128)(2,1)S(1)}, bf16[512,512]{1,0:T(8,128)(2,1)}, u32[]{:S(2)}) copy-start(bf16[512,512]{1,0:T(8,128)(2,1)} %constant.8.x_top.y_top) | copy-start | bytes 1572868
  463.4 26.7 %collective-permute-start.5 = (f32[2,128,256]{2,1,0:T(8,128)S(1)}, f32[2,128,256]{2,1,0:T(8,128)S(1)}, u32[]{:S(2)}, u32[]{:S(2)}) collective-permute-start(f32[2,128,256]{2,1,0:T(8,128)S(1)} %slice.83), channel_id=1, source_target_pairs={{1,0},{2,1},{3,2},{4,3},{5,4},{6,5},{7,6},{0,7},{9,8},{10,9},{11,1... | collective-permute-start | bytes 786440 | tf_op jit(solution)/shard_map/ppermute | solution.py:481
  482.1 8.0 %collective-permute-start.4 = (f32[1,128,256]{2,1,0:T(8,128)S(1)}, f32[1,128,256]{2,1,0:T(8,128)S(1)}, u32[]{:S(2)}, u32[]{:S(2)}) collective-permute-start(f32[1,128,256]{2,1,0:T(8,128)S(1)} %slice.82), channel_id=1, source_target_pairs={{0,1},{1,2},{2,3},{3,4},{4,5},{5,6},{6,7},{7,0},{8,9},{9,10},{10,1... | collective-permute-start | bytes 393224 | tf_op jit(solution)/shard_map/ppermute | solution.py:480
  490.1 4.7 collective-permute-start.7
  490.3 4.5 collective-permute-start.6
  490.9 8.5 %copy-start.1 = (f32[256,128]{1,0:T(8,128)S(1)}, f32[256,128]{1,0:T(8,128)}, u32[]{:S(2)}) copy-start(f32[256,128]{1,0:T(8,128)} %values.3) | copy-start | bytes 393220
  490.9 8.5 %copy-start.2 = (f32[256,128]{1,0:T(8,128)S(1)}, f32[256,128]{1,0:T(8,128)}, u32[]{:S(2)}) copy-start(f32[256,128]{1,0:T(8,128)} %noise.1) | copy-start | bytes 393220
  490.9 8.5 %copy-start.4 = (s32[256,128]{1,0:T(8,128)S(1)}, s32[256,128]{1,0:T(8,128)}, u32[]{:S(2)}) copy-start(s32[256,128]{1,0:T(8,128)} %cz.3) | copy-start | bytes 393220
  490.9 8.5 %copy-start.8 = (s32[256]{0:T(256)S(1)}, s32[256]{0:T(256)}, u32[]{:S(2)}) copy-start(s32[256]{0:T(256)} %tile_grid.3) | copy-start | bytes 3076
  490.9 8.5 %copy-start.10 = (s32[256]{0:T(256)S(1)}, s32[256]{0:T(256)}, u32[]{:S(2)}) copy-start(s32[256]{0:T(256)} %counts.3) | copy-start | bytes 3076

commit v3 on v2

--- a/solution.py
+++ b/solution.py
@@ -46,14 +46,8 @@
     return top, (array - top.astype(jnp.float32)).astype(jnp.bfloat16)
 
 
-def split_dot(left, right, dims):
-    left_top, left_rest = halves(left)
-    right_top, right_rest = halves(right)
-
-    def dot(a, b):
-        return lax.dot_general(a, b, (dims, ((), ())), preferred_element_type=jnp.float32)
-
-    return dot(left_top, right_top) + (dot(left_top, right_rest) + dot(left_rest, right_top))
+def product_dot(left, right, dims):
+    return lax.dot_general(left, right, (dims, ((), ())), preferred_element_type=jnp.float32)
 
 
 def box_weights(taps, start, row):
@@ -64,14 +58,40 @@
     return weight
 
 
-def column_weights(taps, start, row, depth):
-    delta = lax.broadcasted_iota(jnp.int32, (depth, start.shape[1]), 0) - start[row : row + 1] + 1
-    delta = jnp.where(delta < 0, delta + depth, delta)
-    delta = jnp.where(delta >= depth, delta - depth, delta)
-    weight = jnp.zeros(delta.shape, jnp.float32)
+PACK = 16
+
+
+def column_positions(start, depth):
+    positions = []
     for offset in range(4):
-        weight = jnp.where(delta == offset, taps[offset][row : row + 1], weight)
-    return weight
+        position = start + (offset - 1)
+        position = jnp.where(position < 0, position + depth, position)
+        positions.append(jnp.where(position >= depth, position - depth, position))
+    return positions
+
+
+def packed_row(array, row, dtype):
+    return jnp.broadcast_to(array[row : row + 1], (PACK, array.shape[1])).astype(dtype)
+
+
+def column_weights(taps, positions, row, cells):
+    top = jnp.zeros(cells.shape, jnp.bfloat16)
+    rest = jnp.zeros(cells.shape, jnp.bfloat16)
+    for offset in range(4):
+        here = cells == packed_row(positions[offset], row, jnp.int16)[None]
+        first = taps[offset].astype(jnp.bfloat16).astype(jnp.float32)
+        top = jnp.where(here, packed_row(first, row, jnp.bfloat16)[None], top)
+        second = taps[offset] - first
+        rest = jnp.where(here, packed_row(second, row, jnp.bfloat16)[None], rest)
+    flat = (cells.shape[0] * PACK, cells.shape[2])
+    return top.reshape(flat), rest.reshape(flat)
+
+
+def column_cells(depth, points):
+    groups = depth // PACK
+    shape = (groups, PACK, points)
+    cells = lax.broadcasted_iota(jnp.int32, shape, 0) * PACK
+    return (cells + lax.broadcasted_iota(jnp.int32, shape, 1)).astype(jnp.int16)
 
 
 def group_rows(refs, first):
@@ -85,10 +105,13 @@
     points = values.shape[1]
     padded[...] = jnp.zeros_like(padded)
 
+    cells = column_cells(depth, points)
+
     def step(index, carry):
         first = pl.multiple_of(index * GROUP, GROUP)
         value, f0, f1, f2, c0, c1, c2 = group_rows((values, fx, fy, fz, cx, cy, cz), first)
         taps_x, taps_y, taps_z = cubic_taps(f0), cubic_taps(f1), cubic_taps(f2)
+        positions = column_positions(c2, depth)
         slot = lax.broadcasted_iota(jnp.int32, (1, points), 1)
         boxes = []
         for row in range(GROUP):
@@ -96,8 +119,16 @@
             wide_x = box_weights(taps_x, c0, row)
             wide_y = box_weights(taps_y, c1, row) * source
             plane = jnp.concatenate([wide_y[y : y + 1] * wide_x for y in range(SIDE)], 0)
-            column = column_weights(taps_z, c2, row, depth)
-            boxes.append(split_dot(plane, column, ((1,), (1,))))
+            top, rest = column_weights(taps_z, positions, row, cells)
+            plane_top, plane_rest = halves(plane)
+            boxes.append(
+                product_dot(
+                    jnp.concatenate([plane_top, plane_rest], 1),
+                    jnp.concatenate([top, top], 1),
+                    ((1,), (1,)),
+                )
+                + product_dot(plane_top, rest, ((1,), (1,)))
+            )
         for row in range(GROUP):
             owner = tile_grid[first + row]
             at_x = pl.multiple_of((owner // rows_y) * TILE, TILE)
@@ -116,12 +147,15 @@
     depth = field.shape[2]
     points = values.shape[1]
 
+    cells = column_cells(depth, points)
+
     def step(index, carry):
         first = pl.multiple_of(index * GROUP, GROUP)
         value, level, f0, f1, f2, c0, c1, c2 = group_rows(
             (values, noise, fx, fy, fz, cx, cy, cz), first
         )
         taps_x, taps_y, taps_z = cubic_taps(f0), cubic_taps(f1), cubic_taps(f2)
+        positions = column_positions(c2, depth)
         slot = lax.broadcasted_iota(jnp.int32, (1, points), 1)
         rows = []
         for row in range(GROUP):
@@ -129,8 +163,11 @@
             at_x = pl.multiple_of((owner // rows_y) * TILE, TILE)
             at_y = lax.rem(owner, rows_y) * TILE
             box = field[pl.ds(at_y, SIDE), pl.ds(at_x, WINDOW), :].reshape(SIDE * WINDOW, depth)
-            column = column_weights(taps_z, c2, row, depth)
-            along = split_dot(box, column, ((1,), (0,))).reshape(SIDE, WINDOW, points)
+            top, rest = column_weights(taps_z, positions, row, cells)
+            box_top, box_rest = halves(box)
+            both = product_dot(box_top, jnp.concatenate([top, rest], 1), ((1,), (0,)))
+            along = both[:, :points] + both[:, points:] + product_dot(box_rest, top, ((1,), (0,)))
+            along = along.reshape(SIDE, WINDOW, points)
             wide_x = box_weights(taps_x, c0, row)
             wide_y = box_weights(taps_y, c1, row)
             total = along[0] * wide_y[0:1]

time: 545 us -> 512 us (0.939)
  Pallas kernels: 445 us -> 412 us
    pallas_call x1, Pallas kernels: 44.4 us -> 26.7 us  [body(): pl.pallas_call(functools.partial(sample_kernel, rows_y), out_shape=jax.Sh...]
    pallas_call x1, Pallas kernels: 44.9 us -> 30.1 us  [body(): pl.pallas_call(functools.partial(spread_kernel, rows_y), out_shape=jax.Sh...]
where the time goes in v3:
time: 512 us; the launch traced here: 511 us
  Pallas kernels  412 us (80%)
  local copies, waits for them, and re-layouts  30.8 us (6%)
  starting transfers between devices  26.6 us (5%)
  matrix products  18.5 us (4%)
  waiting for transfers between devices  13.9 us (3%)
  other arithmetic  8.71 us (2%)
    pallas_call x1, Pallas kernels, smooth_planes(): pl.pallas_call(functools.partial(planes_kernel, ranks_x, ranks_y, chunks,...  356 us
    pallas_call x1, Pallas kernels, body(): pl.pallas_call(functools.partial(spread_kernel, rows_y), out_shape=jax.Sh...  30.1 us
    pallas_call x1, Pallas kernels, body(): pl.pallas_call(functools.partial(sample_kernel, rows_y), out_shape=jax.Sh...  26.7 us
    ppermute x1, starting transfers between devices, body(): high = lax.ppermute(block[:HIGH], 'gy', backward_y)  19.1 us
    dot_general x1, matrix products, body(): block = einsum('kyx,kz->yxz', returned, table_z)  13.8 us
  transfers between devices with their start and end apart: 8, of which 3 were waited for; matrix products, arithmetic and copies ran while one was open for 3% of the time, Pallas kernels for 0%

profile of v3, /device:TPU:0, one launch (start us, length us, event | category | flops | bytes accessed | tf_op | source)
XLA Modules:
  0.0 511.1 jit_solution(2408176535148031836)
XLA Ops:
  0.0 1.0 slice_bitcast_fusion
  1.0 1.1 slice_bitcast_fusion.2
  2.1 0.0 copy-start
  2.1 0.9 copy-done
  3.0 0.9 copy-done.3
  3.9 0.7 copy-done.7
  4.5 0.7 copy-done.9
  5.2 30.1 %spread.1 = f32[67,136,256]{2,1,0:T(8,128)} custom-call(s32[256]{0:T(256)S(1)} %copy-done.7, s32[256]{0:T(256)S(1)} %copy-done.9, f32[256,128]{1,0:T(8,128)S(1)} %copy-done, f32[256,128]{1,0:T(8,128)S(1)} %get-tuple-element.6.fx, f32[256,128]{1,0:T(8,128)S(1)} %get-tuple-element.7.fy, f32[256,128]{1,0:T(8,128)S(1)} %get-tuple-element.5.fz, ...), custom_call_target="tpu_custom_call" | custom-call | flops 8858370048 | bytes 9330688 | tf_op jit(solution)/shard_map/spread/pallas_call | solution.py:476
  35.3 0.9 slice.80
  36.3 6.0 %collective-permute-start.1 = (f32[1,136,256]{2,1,0:T(8,128)S(1)}, f32[1,136,256]{2,1,0:T(8,128)S(1)}, u32[]{:S(2)}, u32[]{:S(2)}) collective-permute-start(f32[1,136,256]{2,1,0:T(8,128)S(1)} %slice.80), channel_id=1, source_target_pairs={{1,0},{2,1},{3,2},{4,3},{5,4},{6,5},{7,6},{0,7},{9,8},{10,9},{11,1... | collective-permute-start | bytes 417800 | tf_op jit(solution)/shard_map/ppermute | solution.py:489
  42.2 1.0 slice.77
  43.2 0.0 copy-start.15
  43.2 0.1 collective-permute-start
  43.3 7.3 %slice.78 = f32[61,136,256]{2,1,0:T(8,128)} slice(f32[67,136,256]{2,1,0:T(8,128)} %spread.1), slice={[3:64], [0:136], [0:256]} | slice | bytes 16990208 | tf_op jit(solution)/shard_map/slice | solution.py:493
  50.6 0.1 copy.15.rate_y
  50.8 0.0 collective-permute-done.1
  50.8 1.1 slice_add_fusion.1
  51.9 2.2 collective-permute-done
  54.1 1.0 slice_add_fusion
  55.1 1.1 pad_maximum_fusion.5
  56.2 0.7 pad_maximum_fusion
  56.8 0.1 collective-permute-start.3
  56.9 0.1 pad_maximum_fusion.3
  57.0 0.7 collective-permute-start.2
  57.7 4.6 slice.81
  62.3 0.1 maximum_add_fusion.1
  62.4 0.1 maximum_add_fusion
  62.5 2.0 slice-done
  64.5 0.0 copy-done.14
  64.5 1.4 slice-done.1
  65.8 4.7 fusion
  70.6 0.0 copy-start.5
  70.6 0.0 copy-start.6
  70.6 0.0 copy-start.11
  70.6 0.0 copy-start.12
  70.6 8.1 %copy.17.turned = f32[256,64,128]{2,1,0:T(8,128)} copy(f32[256,64,128]{2,0,1:T(8,128)S(1)} %fusion) | data formatting | bytes 16777216 | tf_op jit(solution)/shard_map/kz,yxz->kyx/dot_general | solution.py:513
  78.8 355.6 %smooth.1 = f32[256,64,128]{2,1,0:T(8,128)} custom-call(f32[256]{0:T(256)S(1)} %copy-done.6, f32[1,512]{1,0:T(1,128)S(1)} %bitcast.15, f32[512,1]{1,0:T(8,128)S(1)} %copy.15.rate_y, bf16[512,512]{1,0:T(8,128)(2,1)S(1)} %copy-done.12, bf16[512,512]{1,0:T(8,128)(2,1)S(1)} %copy-done.11, bf16[512,512]{1,0:T(8,128)(2,1)S(1)} %copy-done.12, ...), custom_call_target="tpu_custom_call" | custom-call | flops 51539607552 | bytes 16777216 | tf_op jit(solution)/shard_map/smooth/pallas_call | solution.py:427
  434.4 13.8 %fusion.6 = f32[64,128,256]{2,1,0:T(8,128)S(1)} fusion(f32[256,256,1]{1,0,2:T(8,128)S(1)} %copy-done.14, f32[256,64,128]{2,1,0:T(8,128)} %smooth.1), kind=kOutput, calls=%fused_computation.8 | convolution fusion | flops 3221225472 | bytes 17039360 | tf_op jit(solution)/shard_map/kyx,kz->yxz/dot_general | solution.py:515
  448.2 19.1 %collective-permute-start.5 = (f32[2,128,256]{2,1,0:T(8,128)S(1)}, f32[2,128,256]{2,1,0:T(8,128)S(1)}, u32[]{:S(2)}, u32[]{:S(2)}) collective-permute-start(f32[2,128,256]{2,1,0:T(8,128)S(1)} %slice.83), channel_id=1, source_target_pairs={{1,0},{2,1},{3,2},{4,3},{5,4},{6,5},{7,6},{0,7},{9,8},{10,9},{11,1... | collective-permute-start | bytes 786440 | tf_op jit(solution)/shard_map/ppermute | solution.py:518
  467.3 0.1 collective-permute-start.4
  467.4 7.9 %collective-permute-done.4 = f32[1,128,256]{2,1,0:T(8,128)S(1)} collective-permute-done((f32[1,128,256]{2,1,0:T(8,128)S(1)}, f32[1,128,256]{2,1,0:T(8,128)S(1)}, u32[]{:S(2)}, u32[]{:S(2)}) %collective-permute-start.4) | collective-permute-done | bytes 131104 | tf_op jit(solution)/shard_map/ppermute | solution.py:517
  475.3 0.1 collective-permute-start.7
  475.4 0.1 pad_maximum_fusion.4
  475.5 0.5 collective-permute-start.6
  476.0 0.1 pad.5.clone
  476.1 3.7 collective-permute-done.6
  479.9 4.6 maximum_maximum_fusion.field
  484.4 26.7 %sample.1 = f32[256,128]{1,0:T(8,128)} custom-call(s32[256]{0:T(256)S(1)} %copy-done.8, s32[256]{0:T(256)S(1)} %copy-done.10, f32[256,128]{1,0:T(8,128)S(1)} %copy-done.1, f32[256,128]{1,0:T(8,128)S(1)} %copy-done.2, f32[256,128]{1,0:T(8,128)S(1)} %get-tuple-element.6.fx, f32[256,128]{1,0:T(8,128)S(1)} %get-tuple-element.7.fy, ...), custom_call_target="tpu_custom_call" | custom-call | flops 8858370048 | bytes 9330688 | tf_op jit(solution)/shard_map/sample/pallas_call | solution.py:525
  (32 shorter events, 0.1 us)
Async XLA Ops:
  2.1 0.9 copy-start
  3.0 0.9 copy-start.3
  3.9 0.7 copy-start.7
  4.5 0.7 copy-start.9
  36.3 14.5 %collective-permute-start.1 = (f32[1,136,256]{2,1,0:T(8,128)S(1)}, f32[1,136,256]{2,1,0:T(8,128)S(1)}, u32[]{:S(2)}, u32[]{:S(2)}) collective-permute-start(f32[1,136,256]{2,1,0:T(8,128)S(1)} %slice.80), channel_id=1, source_target_pairs={{1,0},{2,1},{3,2},{4,3},{5,4},{6,5},{7,6},{0,7},{9,8},{10,9},{11,1... | collective-permute-start | bytes 417800 | tf_op jit(solution)/shard_map/ppermute | solution.py:489
  43.2 7.4 %copy-start.15 = (f32[512]{0:T(512)S(1)}, f32[512]{0:T(512)}, u32[]{:S(2)}) copy-start(f32[512]{0:T(512)} %param.21) | copy-start | bytes 6148
  43.2 10.9 %collective-permute-start = (f32[2,136,256]{2,1,0:T(8,128)S(1)}, f32[2,136,256]{2,1,0:T(8,128)S(1)}, u32[]{:S(2)}, u32[]{:S(2)}) collective-permute-start(f32[2,136,256]{2,1,0:T(8,128)S(1)} %slice.77), channel_id=1, source_target_pairs={{0,1},{1,2},{2,3},{3,4},{4,5},{5,6},{6,7},{7,0},{8,9},{9,10},{10,1... | collective-permute-start | bytes 835592 | tf_op jit(solution)/shard_map/ppermute | solution.py:488
  50.8 5.4 %copy-start.13 = (f32[61,136,256]{2,1,0:T(8,128)S(1)}, f32[61,136,256]{2,1,0:T(8,128)}, u32[]{:S(2)}) copy-start(f32[61,136,256]{2,1,0:T(8,128)} %slice.78) | copy-start | bytes 25485316
  56.8 5.5 %collective-permute-start.3 = (f32[64,1,256]{2,1,0:T(1,128)S(1)}, f32[64,1,256]{2,1,0:T(1,128)S(1)}, u32[]{:S(2)}, u32[]{:S(2)}) collective-permute-start(f32[64,1,256]{2,1,0:T(1,128)S(1)} %pad_maximum_fusion.5), channel_id=1, source_target_pairs={{8,0},{16,8},{24,16},{0,24},{9,1},{17,9},{25,17},{1,25},{10,2},{18... | collective-permute-start | bytes 196616 | tf_op jit(solution)/shard_map/ppermute | solution.py:501
  57.0 5.4 %collective-permute-start.2 = (f32[64,2,256]{2,1,0:T(2,128)S(1)}, f32[64,2,256]{2,1,0:T(2,128)S(1)}, u32[]{:S(2)}, u32[]{:S(2)}) collective-permute-start(f32[64,2,256]{2,1,0:T(2,128)S(1)} %pad_maximum_fusion.3), channel_id=1, source_target_pairs={{0,8},{8,16},{16,24},{24,0},{1,9},{9,17},{17,25},{25,1},{2,10},{10... | collective-permute-start | bytes 393224 | tf_op jit(solution)/shard_map/ppermute | solution.py:498
  62.3 2.2 slice-start
  62.3 2.2 copy-start.14
  62.4 3.5 slice-start.1
  70.6 8.2 %copy-start.5 = (f32[512]{0:T(512)S(1)}, f32[512]{0:T(512)}, u32[]{:S(2)}) copy-start(f32[512]{0:T(512)} %param.20) | copy-start | bytes 6148
  70.6 8.2 %copy-start.6 = (f32[256]{0:T(256)S(1)}, f32[256]{0:T(256)}, u32[]{:S(2)}) copy-start(f32[256]{0:T(256)} %rate_z.1) | copy-start | bytes 3076
  70.6 8.2 %copy-start.11 = (bf16[512,512]{1,0:T(8,128)(2,1)S(1)}, bf16[512,512]{1,0:T(8,128)(2,1)}, u32[]{:S(2)}) copy-start(bf16[512,512]{1,0:T(8,128)(2,1)} %constant.11.x_rest.y_rest) | copy-start | bytes 1572868
  70.6 8.2 %copy-start.12 = (bf16[512,512]{1,0:T(8,128)(2,1)S(1)}, bf16[512,512]{1,0:T(8,128)(2,1)}, u32[]{:S(2)}) copy-start(bf16[512,512]{1,0:T(8,128)(2,1)} %constant.8.x_top.y_top) | copy-start | bytes 1572868
  448.2 27.1 %collective-permute-start.5 = (f32[2,128,256]{2,1,0:T(8,128)S(1)}, f32[2,128,256]{2,1,0:T(8,128)S(1)}, u32[]{:S(2)}, u32[]{:S(2)}) collective-permute-start(f32[2,128,256]{2,1,0:T(8,128)S(1)} %slice.83), channel_id=1, source_target_pairs={{1,0},{2,1},{3,2},{4,3},{5,4},{6,5},{7,6},{0,7},{9,8},{10,9},{11,1... | collective-permute-start | bytes 786440 | tf_op jit(solution)/shard_map/ppermute | solution.py:518
  467.3 8.0 %collective-permute-start.4 = (f32[1,128,256]{2,1,0:T(8,128)S(1)}, f32[1,128,256]{2,1,0:T(8,128)S(1)}, u32[]{:S(2)}, u32[]{:S(2)}) collective-permute-start(f32[1,128,256]{2,1,0:T(8,128)S(1)} %slice.82), channel_id=1, source_target_pairs={{0,1},{1,2},{2,3},{3,4},{4,5},{5,6},{6,7},{7,0},{8,9},{9,10},{10,1... | collective-permute-start | bytes 393224 | tf_op jit(solution)/shard_map/ppermute | solution.py:517
  475.3 4.5 collective-permute-start.7
  475.5 4.4 collective-permute-start.6
  476.1 8.3 %copy-start.1 = (f32[256,128]{1,0:T(8,128)S(1)}, f32[256,128]{1,0:T(8,128)}, u32[]{:S(2)}) copy-start(f32[256,128]{1,0:T(8,128)} %values.3) | copy-start | bytes 393220
  476.1 8.3 %copy-start.2 = (f32[256,128]{1,0:T(8,128)S(1)}, f32[256,128]{1,0:T(8,128)}, u32[]{:S(2)}) copy-start(f32[256,128]{1,0:T(8,128)} %noise.1) | copy-start | bytes 393220
  476.1 8.3 %copy-start.4 = (s32[256,128]{1,0:T(8,128)S(1)}, s32[256,128]{1,0:T(8,128)}, u32[]{:S(2)}) copy-start(s32[256,128]{1,0:T(8,128)} %cz.3) | copy-start | bytes 393220
  476.1 8.3 %copy-start.8 = (s32[256]{0:T(256)S(1)}, s32[256]{0:T(256)}, u32[]{:S(2)}) copy-start(s32[256]{0:T(256)} %tile_grid.3) | copy-start | bytes 3076
  476.1 8.3 %copy-start.10 = (s32[256]{0:T(256)S(1)}, s32[256]{0:T(256)}, u32[]{:S(2)}) copy-start(s32[256]{0:T(256)} %counts.3) | copy-start | bytes 3076

commit v4 on v3

--- a/solution.py
+++ b/solution.py
@@ -99,7 +99,8 @@
 
 
 def spread_kernel(
-    rows_y, tile_grid, counts, values, fx, fy, fz, cx, cy, cz, padded
+    rows_y, tile_grid, counts, values, fx, fy, fz, cx, cy, cz,
+    block, y_low, y_high, x_low, x_high, padded,
 ):
     depth = padded.shape[2]
     points = values.shape[1]
@@ -139,11 +140,42 @@
         return carry
 
     lax.fori_loop(0, values.shape[0] // GROUP, step, 0)
+    cells_y, cells_x = block.shape[0], block.shape[1]
+
+    def move(row, carry):
+        block[row] = padded[row + LOW, LOW : cells_x + LOW, :]
+        x_low[row] = padded[row + LOW, :LOW, :]
+        x_high[row] = padded[row + LOW, cells_x + LOW : cells_x + LOW + HIGH, :]
+        return carry
+
+    lax.fori_loop(0, cells_y, move, 0)
+    y_low[...] = padded[:LOW]
+    y_high[...] = padded[cells_y + LOW :]
 
 
 def sample_kernel(
-    rows_y, tile_grid, counts, values, noise, fx, fy, fz, cx, cy, cz, field, product
+    rows_y, tile_grid, counts, values, noise, fx, fy, fz, cx, cy, cz,
+    block, y_low, y_high, x_low, x_high, product, field,
 ):
+    cells_y, cells_x = block.shape[0], block.shape[1]
+
+    def move(row, carry):
+        field[row + LOW, LOW : cells_x + LOW, :] = block[row]
+        return carry
+
+    lax.fori_loop(0, cells_y, move, 0)
+    field[:LOW, LOW : cells_x + LOW, :] = y_low[...]
+    field[cells_y + LOW :, LOW : cells_x + LOW, :] = y_high[...]
+
+    def border(row, carry):
+        field[row, :LOW, :] = x_low[row]
+        field[row, cells_x + LOW : cells_x + LOW + HIGH, :] = x_high[row]
+        field[row, cells_x + LOW + HIGH :, :] = jnp.zeros(
+            (field.shape[1] - cells_x - LOW - HIGH, field.shape[2]), jnp.float32
+        )
+        return carry
+
+    lax.fori_loop(0, field.shape[0], border, 0)
     depth = field.shape[2]
     points = values.shape[1]
 
@@ -473,11 +505,21 @@
     cost = pl.CostEstimate(
         flops=flops, bytes_accessed=4 * wide_x * wide_y * depth, transcendentals=0
     )
-    padded = pl.pallas_call(
+    block, y_low, y_high, x_low, x_high = pl.pallas_call(
         functools.partial(spread_kernel, rows_y),
-        out_shape=jax.ShapeDtypeStruct((wide_y, wide_x, depth), jnp.float32),
+        out_shape=[
+            jax.ShapeDtypeStruct(shape, jnp.float32)
+            for shape in (
+                (cells_y, cells_x, depth),
+                (LOW, wide_x, depth),
+                (HIGH, wide_x, depth),
+                (cells_y, LOW, depth),
+                (cells_y, HIGH, depth),
+            )
+        ],
         in_specs=[smem, smem] + [vmem] * 7,
-        out_specs=vmem,
+        out_specs=[vmem] * 5,
+        scratch_shapes=[pltpu.VMEM((wide_y, wide_x, depth), jnp.float32)],
         compiler_params=params,
         cost_estimate=cost,
         name="spread",
@@ -485,28 +527,20 @@
 
     forward_x, backward_x = ring("gx")
     forward_y, backward_y = ring("gy")
-    from_low = lax.ppermute(padded[cells_y + LOW :], "gy", forward_y)
-    from_high = lax.ppermute(padded[:LOW], "gy", backward_y)
-    padded = jnp.concatenate(
-        [
-            padded[LOW : LOW + HIGH] + from_low,
-            padded[LOW + HIGH : cells_y],
-            padded[cells_y : cells_y + LOW] + from_high,
-        ],
-        0,
-    )
-    from_low = lax.ppermute(
-        padded[:, cells_x + LOW : cells_x + LOW + HIGH], "gx", forward_x
-    )
-    from_high = lax.ppermute(padded[:, :LOW], "gx", backward_x)
-    spread_grid = jnp.concatenate(
-        [
-            padded[:, LOW : LOW + HIGH] + from_low,
-            padded[:, LOW + HIGH : cells_x],
-            padded[:, cells_x : cells_x + LOW] + from_high,
-        ],
-        1,
-    )
+    from_low = lax.ppermute(y_high, "gy", forward_y)
+    from_high = lax.ppermute(y_low, "gy", backward_y)
+
+    def with_edges(part, first, last):
+        part = part.at[:HIGH].add(from_low[:, first:last])
+        return part.at[cells_y - LOW :].add(from_high[:, first:last])
+
+    inner = cells_x + LOW
+    block = with_edges(block, LOW, inner)
+    x_low = with_edges(x_low, 0, LOW)
+    x_high = with_edges(x_high, inner, inner + HIGH)
+    from_low = lax.ppermute(x_high, "gx", forward_x)
+    from_high = lax.ppermute(x_low, "gx", backward_x)
+    spread_grid = block.at[:, :HIGH].add(from_low).at[:, cells_x - LOW :].add(from_high)
 
     table_z = cas_table(depth)
     einsum = functools.partial(jnp.einsum, precision=lax.Precision.HIGH)
@@ -514,23 +548,27 @@
     returned = smooth_planes(turned, rate_x, rate_y, rate_z, ranks_x, ranks_y)
     block = einsum("kyx,kz->yxz", returned, table_z)
 
-    low = lax.ppermute(block[cells_y - LOW :], "gy", forward_y)
-    high = lax.ppermute(block[:HIGH], "gy", backward_y)
-    block = jnp.concatenate([low, block, high], 0)
-    low = lax.ppermute(block[:, cells_x - LOW :], "gx", forward_x)
-    high = lax.ppermute(block[:, :HIGH], "gx", backward_x)
-    spare = jnp.zeros((wide_y, TILE - LOW - HIGH, depth), jnp.float32)
-    field = jnp.concatenate([low, block, high, spare], 1)
+    y_low = lax.ppermute(block[cells_y - LOW :], "gy", forward_y)
+    y_high = lax.ppermute(block[:HIGH], "gy", backward_y)
+
+    def column(first, last):
+        return jnp.concatenate([part[:, first:last] for part in (y_low, block, y_high)], 0)
+
+    x_low = lax.ppermute(column(cells_x - LOW, cells_x), "gx", forward_x)
+    x_high = lax.ppermute(column(0, HIGH), "gx", backward_x)
 
     return pl.pallas_call(
         functools.partial(sample_kernel, rows_y),
         out_shape=jax.ShapeDtypeStruct((tile_count, point_count), jnp.float32),
-        in_specs=[smem, smem] + [vmem] * 9,
+        in_specs=[smem, smem] + [vmem] * 13,
         out_specs=vmem,
+        scratch_shapes=[pltpu.VMEM((wide_y, wide_x, depth), jnp.float32)],
         compiler_params=params,
         cost_estimate=cost,
         name="sample",
-    )(tile_grid, counts, values, noise, *places, field)
+    )(
+        tile_grid, counts, values, noise, *places, block, y_low, y_high, x_low, x_high
+    )
 
 
 def solution(mesh):

time: 512 us -> 504 us (0.984)
  local copies, waits for them, and re-layouts: 30.8 us -> 16.1 us
  waiting for transfers between devices: 13.9 us -> 19.4 us
    slice x6 -> x8, local copies, waits for them, and re-layouts: 13.8 us -> 0.15 us  [the longest x6 0.12 us: column(): part[:, first:last]]
    ppermute x8, waiting for transfers between devices: 13.9 us -> 19.4 us  [the longest x1 7.53 us: body(): y_low = lax.ppermute(block[cells_y - LOW:], 'gy', forward_y)]
    concatenate x3 -> x2, other arithmetic: 5.27 us -> 0.12 us  [column(): jnp.concatenate([part[:, first:last] for part in (y_low, block, y_high)], 0)]
  transfers between devices with their start and end apart: 8 -> 8, of which waited for: 3 -> 4; matrix products, arithmetic and copies ran while one was open for 3% -> 1% of each run, Pallas kernels for 0% -> 0%
where the time goes in v4:
time: 504 us; the launch traced here: 503 us
  Pallas kernels  413 us (82%)
  starting transfers between devices  27.8 us (6%)
  matrix products  20.1 us (4%)
  waiting for transfers between devices  19.4 us (4%)
  local copies, waits for them, and re-layouts  16.1 us (3%)
  other arithmetic  6.36 us (1%)
    pallas_call x1, Pallas kernels, smooth_planes(): pl.pallas_call(functools.partial(planes_kernel, ranks_x, ranks_y, chunks,...  355 us
    pallas_call x1, Pallas kernels, body(): pl.pallas_call(functools.partial(spread_kernel, rows_y), out_shape=[jax.S...  30.8 us
    pallas_call x1, Pallas kernels, body(): pl.pallas_call(functools.partial(sample_kernel, rows_y), out_shape=jax.Sh...  27.8 us
    ppermute x1, starting transfers between devices, body(): y_high = lax.ppermute(block[:HIGH], 'gy', backward_y)  19.3 us
    dot_general x1, matrix products, body(): block = einsum('kyx,kz->yxz', returned, table_z)  14 us
  transfers between devices with their start and end apart: 8, of which 4 were waited for; matrix products, arithmetic and copies ran while one was open for 1% of the time, Pallas kernels for 0%

profile of v4, /device:TPU:0, one launch (start us, length us, event | category | flops | bytes accessed | tf_op | source)
XLA Modules:
  0.0 503.2 jit_solution(6599493198584476551)
XLA Ops:
  0.0 1.1 slice_bitcast_fusion.2
  1.1 1.0 slice_bitcast_fusion
  2.1 0.0 copy-start
  2.1 0.9 copy-done
  3.0 0.9 copy-done.3
  3.9 0.7 copy-done.7
  4.5 0.7 copy-done.9
  5.2 30.8 %spread.1 = (f32[64,128,256]{2,1,0:T(8,128)}, f32[1,136,256]{2,1,0:T(8,128)S(1)}, f32[2,136,256]{2,1,0:T(8,128)S(1)}, f32[64,1,256]{2,1,0:T(1,128)S(1)}, f32[64,2,256]{2,1,0:T(2,128)S(1)}) custom-call(s32[256]{0:T(256)S(1)} %copy-done.7, s32[256]{0:T(256)S(1)} %copy-done.9, f32[256,128]{1,0:T(8,128)S(1)} %copy-done, f32[256,128]{1,0:T(8,128)S(1)} %get-tuple-element.112.fx, ...), custom_call_target="tpu_custom_call" | custom-call | flops 8858370048 | bytes 9330688 | tf_op jit(solution)/shard_map/spread/pallas_call | solution.py:508
  36.0 3.1 collective-permute-start
  39.1 2.9 collective-permute-start.1
  42.0 0.1 copy.15.rate_y
  42.2 6.6 %collective-permute-done = f32[2,136,256]{2,1,0:T(8,128)S(1)} collective-permute-done((f32[2,136,256]{2,1,0:T(8,128)S(1)}, f32[2,136,256]{2,1,0:T(8,128)S(1)}, u32[]{:S(2)}, u32[]{:S(2)}) %collective-permute-start) | collective-permute-done | bytes 278560 | tf_op jit(solution)/shard_map/ppermute | solution.py:530
  48.8 1.3 collective-permute-done.1
  50.1 0.0 collective-permute-start.2
  50.2 1.8 collective-permute-start.3
  51.9 1.7 fusion.2
  53.6 1.6 fusion.4
  55.2 0.0 collective-permute-done.2
  55.2 1.8 fusion.3
  57.0 0.0 collective-permute-done.3
  57.0 1.1 slice_add_fusion.3
  58.1 2.4 scatter-add.39
  60.5 6.1 %fusion.8 = f32[256,64,128]{2,0,1:T(8,128)S(1)} fusion(f32[256,256,1]{1,0,2:T(8,128)S(1)} %copy-done.14, f32[64,128,256]{2,1,0:T(8,128)} %scatter-add.39), kind=kOutput, calls=%fused_computation.24 | convolution fusion | flops 3221225472 | bytes 17039360 | tf_op jit(solution)/shard_map/kz,yxz->kyx/dot_general | solution.py:547
  66.6 0.0 copy-start.5
  66.7 0.0 copy-start.6
  66.7 0.0 copy-start.11
  66.7 0.0 copy-start.12
  66.7 8.1 %copy.17.turned = f32[256,64,128]{2,1,0:T(8,128)} copy(f32[256,64,128]{2,0,1:T(8,128)S(1)} %fusion.8) | data formatting | bytes 16777216 | tf_op jit(solution)/shard_map/kz,yxz->kyx/dot_general | solution.py:547
  74.8 0.0 copy-done.11
  74.8 354.6 %smooth.1 = f32[256,64,128]{2,1,0:T(8,128)} custom-call(f32[256]{0:T(256)S(1)} %copy-done.6, f32[1,512]{1,0:T(1,128)S(1)} %bitcast.16, f32[512,1]{1,0:T(8,128)S(1)} %copy.15.rate_y, bf16[512,512]{1,0:T(8,128)(2,1)S(1)} %copy-done.11, bf16[512,512]{1,0:T(8,128)(2,1)S(1)} %copy-done.12, bf16[512,512]{1,0:T(8,128)(2,1)S(1)} %copy-done.11, ...), custom_call_target="tpu_custom_call" | custom-call | flops 51539607552 | bytes 16777216 | tf_op jit(solution)/shard_map/smooth/pallas_call | solution.py:459
  429.5 0.0 copy-start.1
  429.5 0.0 copy-start.2
  429.5 0.0 copy-start.4
  429.5 0.0 copy-start.8
  429.5 0.0 copy-start.10
  429.5 14.0 %fusion.block = f32[64,128,256]{2,1,0:T(8,128)S(1)} fusion(f32[256,256,1]{1,0,2:T(8,128)S(1)} %copy-done.14, f32[256,64,128]{2,1,0:T(8,128)} %smooth.1), kind=kOutput, calls=%fused_computation | convolution fusion | flops 3221225472 | bytes 17039360 | tf_op jit(solution)/shard_map/kyx,kz->yxz/dot_general | solution.py:549
  443.6 19.3 %collective-permute-start.5 = (f32[2,128,256]{2,1,0:T(8,128)S(1)}, f32[2,128,256]{2,1,0:T(8,128)S(1)}, u32[]{:S(2)}, u32[]{:S(2)}) collective-permute-start(f32[2,128,256]{2,1,0:T(8,128)S(1)} %slice.288), channel_id=1, source_target_pairs={{1,0},{2,1},{3,2},{4,3},{5,4},{6,5},{7,6},{0,7},{9,8},{10,9},{11,1... | collective-permute-start | bytes 786440 | tf_op jit(solution)/shard_map/ppermute | solution.py:552
  462.9 0.1 collective-permute-start.4
  463.0 0.1 slice.290
  463.1 7.5 %collective-permute-done.4.y_low = f32[1,128,256]{2,1,0:T(8,128)S(1)} collective-permute-done((f32[1,128,256]{2,1,0:T(8,128)S(1)}, f32[1,128,256]{2,1,0:T(8,128)S(1)}, u32[]{:S(2)}, u32[]{:S(2)}) %collective-permute-start.4) | collective-permute-done | bytes 131104 | tf_op jit(solution)/shard_map/ppermute | solution.py:551
  470.6 0.0 collective-permute-done.5.y_high
  470.7 0.1 pad_maximum_fusion
  470.7 0.1 collective-permute-start.7
  470.8 0.1 pad_maximum_fusion.1
  470.9 0.5 collective-permute-start.6
  471.4 3.9 collective-permute-done.6.x_low
  475.3 0.0 collective-permute-done.7.x_high
  475.4 27.8 %sample.1 = f32[256,128]{1,0:T(8,128)} custom-call(s32[256]{0:T(256)S(1)} %copy-done.8, s32[256]{0:T(256)S(1)} %copy-done.10, f32[256,128]{1,0:T(8,128)S(1)} %copy-done.1, f32[256,128]{1,0:T(8,128)S(1)} %copy-done.2, f32[256,128]{1,0:T(8,128)S(1)} %get-tuple-element.112.fx, f32[256,128]{1,0:T(8,128)S(1)} %get-tuple-element.113.fy, ...), custom_call_target="tpu_custom_call" | custom-call | flops 8858370048 | bytes 9330688 | tf_op jit(solution)/shard_map/sample/pallas_call | solution.py:560
  (28 shorter events, 0.2 us)
Async XLA Ops:
  2.1 0.9 copy-start
  3.0 0.9 copy-start.3
  3.9 0.7 copy-start.7
  4.5 0.7 copy-start.9
  5.2 36.8 %copy-start.15 = (f32[512]{0:T(512)S(1)}, f32[512]{0:T(512)}, u32[]{:S(2)}) copy-start(f32[512]{0:T(512)} %param.37) | copy-start | bytes 6148
  5.2 55.3 %copy-start.14 = (f32[256,256,1]{1,0,2:T(8,128)S(1)}, f32[256,256,1]{1,0,2:T(8,128)}, u32[]{:S(2)}) copy-start(f32[256,256,1]{1,0,2:T(8,128)} %constant.198) | copy-start | bytes 786436
  36.0 12.7 %collective-permute-start = (f32[2,136,256]{2,1,0:T(8,128)S(1)}, f32[2,136,256]{2,1,0:T(8,128)S(1)}, u32[]{:S(2)}, u32[]{:S(2)}) collective-permute-start(f32[2,136,256]{2,1,0:T(8,128)S(1)} %get-tuple-element.107), channel_id=1, source_target_pairs={{0,1},{1,2},{2,3},{3,4},{4,5},{5,6},{6,7},{7,0},{8,9},{9,10},{10,1... | collective-permute-start | bytes 835592 | tf_op jit(solution)/shard_map/ppermute | solution.py:530
  39.1 11.0 %collective-permute-start.1 = (f32[1,136,256]{2,1,0:T(8,128)S(1)}, f32[1,136,256]{2,1,0:T(8,128)S(1)}, u32[]{:S(2)}, u32[]{:S(2)}) collective-permute-start(f32[1,136,256]{2,1,0:T(8,128)S(1)} %get-tuple-element.108), channel_id=1, source_target_pairs={{1,0},{2,1},{3,2},{4,3},{5,4},{6,5},{7,6},{0,7},{9,8},{10,9},{11,1... | collective-permute-start | bytes 417800 | tf_op jit(solution)/shard_map/ppermute | solution.py:531
  50.1 5.1 %collective-permute-start.2 = (f32[64,2,256]{2,1,0:T(2,128)S(1)}, f32[64,2,256]{2,1,0:T(2,128)S(1)}, u32[]{:S(2)}, u32[]{:S(2)}) collective-permute-start(f32[64,2,256]{2,1,0:T(2,128)S(1)} %fusion.7), channel_id=1, source_target_pairs={{0,8},{8,16},{16,24},{24,0},{1,9},{9,17},{17,25},{25,1},{2,10},{10... | collective-permute-start | bytes 393224 | tf_op jit(solution)/shard_map/ppermute | solution.py:541
  50.2 6.8 %collective-permute-start.3 = (f32[64,1,256]{2,1,0:T(1,128)S(1)}, f32[64,1,256]{2,1,0:T(1,128)S(1)}, u32[]{:S(2)}, u32[]{:S(2)}) collective-permute-start(f32[64,1,256]{2,1,0:T(1,128)S(1)} %constant_dynamic-update-slice_fusion), channel_id=1, source_target_pairs={{8,0},{16,8},{24,16},{0,24},{9,1},{17,9},{25,17},{1,25},{10,2},{18... | collective-permute-start | bytes 196616 | tf_op jit(solution)/shard_map/ppermute | solution.py:542
  66.6 8.2 %copy-start.5 = (f32[512]{0:T(512)S(1)}, f32[512]{0:T(512)}, u32[]{:S(2)}) copy-start(f32[512]{0:T(512)} %param.36) | copy-start | bytes 6148
  66.7 8.2 %copy-start.6 = (f32[256]{0:T(256)S(1)}, f32[256]{0:T(256)}, u32[]{:S(2)}) copy-start(f32[256]{0:T(256)} %rate_z.1) | copy-start | bytes 3076
  66.7 8.2 %copy-start.11 = (bf16[512,512]{1,0:T(8,128)(2,1)S(1)}, bf16[512,512]{1,0:T(8,128)(2,1)}, u32[]{:S(2)}) copy-start(bf16[512,512]{1,0:T(8,128)(2,1)} %constant.194.x_top.y_top) | copy-start | bytes 1572868
  66.7 8.2 %copy-start.12 = (bf16[512,512]{1,0:T(8,128)(2,1)S(1)}, bf16[512,512]{1,0:T(8,128)(2,1)}, u32[]{:S(2)}) copy-start(bf16[512,512]{1,0:T(8,128)(2,1)} %constant.197.x_rest.y_rest) | copy-start | bytes 1572868
  429.5 45.9 %copy-start.1 = (f32[256,128]{1,0:T(8,128)S(1)}, f32[256,128]{1,0:T(8,128)}, u32[]{:S(2)}) copy-start(f32[256,128]{1,0:T(8,128)} %values.3) | copy-start | bytes 393220
  429.5 45.9 %copy-start.2 = (f32[256,128]{1,0:T(8,128)S(1)}, f32[256,128]{1,0:T(8,128)}, u32[]{:S(2)}) copy-start(f32[256,128]{1,0:T(8,128)} %noise.1) | copy-start | bytes 393220
  429.5 45.9 %copy-start.4 = (s32[256,128]{1,0:T(8,128)S(1)}, s32[256,128]{1,0:T(8,128)}, u32[]{:S(2)}) copy-start(s32[256,128]{1,0:T(8,128)} %cz.3) | copy-start | bytes 393220
  429.5 45.9 %copy-start.8 = (s32[256]{0:T(256)S(1)}, s32[256]{0:T(256)}, u32[]{:S(2)}) copy-start(s32[256]{0:T(256)} %tile_grid.3) | copy-start | bytes 3076
  429.5 45.9 %copy-start.10 = (s32[256]{0:T(256)S(1)}, s32[256]{0:T(256)}, u32[]{:S(2)}) copy-start(s32[256]{0:T(256)} %counts.3) | copy-start | bytes 3076
  443.5 31.8 %copy-start.13 = (f32[64,128,256]{2,1,0:T(8,128)}, f32[64,128,256]{2,1,0:T(8,128)S(1)}, u32[]{:S(2)}) copy-start(f32[64,128,256]{2,1,0:T(8,128)S(1)} %fusion.block) | copy-start | bytes 25165828
  443.6 27.1 %collective-permute-start.5 = (f32[2,128,256]{2,1,0:T(8,128)S(1)}, f32[2,128,256]{2,1,0:T(8,128)S(1)}, u32[]{:S(2)}, u32[]{:S(2)}) collective-permute-start(f32[2,128,256]{2,1,0:T(8,128)S(1)} %slice.288), channel_id=1, source_target_pairs={{1,0},{2,1},{3,2},{4,3},{5,4},{6,5},{7,6},{0,7},{9,8},{10,9},{11,1... | collective-permute-start | bytes 786440 | tf_op jit(solution)/shard_map/ppermute | solution.py:552
  462.9 7.7 %collective-permute-start.4 = (f32[1,128,256]{2,1,0:T(8,128)S(1)}, f32[1,128,256]{2,1,0:T(8,128)S(1)}, u32[]{:S(2)}, u32[]{:S(2)}) collective-permute-start(f32[1,128,256]{2,1,0:T(8,128)S(1)} %slice.287), channel_id=1, source_target_pairs={{0,1},{1,2},{2,3},{3,4},{4,5},{5,6},{6,7},{7,0},{8,9},{9,10},{10,1... | collective-permute-start | bytes 393224 | tf_op jit(solution)/shard_map/ppermute | solution.py:551
  470.7 4.6 collective-permute-start.7
  470.9 4.5 collective-permute-start.6
